TPU v7x, 256 devices: a whole 4x4x8 slice. The times are simulated.
256 devices in a mesh: ctx: 16 (over z, y_lo), req: 16 (over x, y_hi, core).
Axes of the slice: x: 4, y: 4 (y_hi: 2, y_lo: 2; y = y_hi * 2 + y_lo), z: 8, core: 2. Of those that a mesh axis runs over, the one named last changes fastest.
Arguments:
- hidden_in: bfloat16 [1024, 4608], P('req'), may hold values from -6 to 6
- queries: bfloat16 [1024, 4096], P('req'), may hold values from -6 to 6
- suffix_kv: bfloat16 [2, 1024, 2048], P(None, 'req'), may hold values from -6 to 6
- prefix_kv: bfloat16 [2, 32, 2048, 2048], P(None, 'req', 'ctx'), may hold values from -6 to 6
- hyp_prefix: int32 [64], P('req'), may hold values from 0 to 31, as said below
- suffix_len: int32 [64], P('req'), may hold values from 1 to 16
- prefix_len: int32 [32], P('req'), may hold values from 1 to 2048
- w_out: bfloat16 [4096, 4608], P('ctx'), may hold values from -0.09375 to 0.09375
- gain_attn: float32 [4608], replicated, may hold values from 0.25 to 1.75
- gain_pre: float32 [4608], replicated, may hold values from 0.25 to 1.75
- w_gate: bfloat16 [4608, 36864], P(None, ('req', 'ctx')), may hold values from -0.09375 to 0.09375
- w_up: bfloat16 [4608, 36864], P(None, ('req', 'ctx')), may hold values from -0.09375 to 0.09375
- w_down: bfloat16 [36864, 4608], P('req', 'ctx'), may hold values from -0.03125 to 0.03125
Outputs:
- resid: bfloat16 [1024, 4608], P('req')
- ffn_out: bfloat16 [1024, 4608], P('req', 'ctx')
Inputs may be any that keep to these rules, and one draw needn't show every extreme that they name: `hyp_prefix`: hypothesis h continues a prefix of its own request group, one of (h // 4) * 2 to (h // 4) * 2 + 1.
All inputs are finite; a program needn't handle non-finite values.
Results may differ from a plain program's by a relative error of at most 0.012.
Values may be sent and summed in bfloat16 or wider, within the bound.
A program may use at most 64 MiB of HBM per device.

v0:
```python
import jax
import jax.numpy as jnp
from jax import lax
from jax.sharding import PartitionSpec as P

HEADS = 32
KV_HEADS = 16
HEAD = 128


softcap = 50.0
query_scale = 144.0 ** (-0.5)
eps = 1e-06


def prefix_terms(key_block, value_block, first, query_part, token_pid, prefix_len):
    prefix_count = key_block.shape[0]
    row_count = key_block.shape[1]
    head_count = key_block.shape[2]
    flat_keys = key_block.reshape(prefix_count * row_count, head_count, HEAD)
    flat_vals = value_block.reshape(prefix_count * row_count, head_count, HEAD)
    scores = (
        jnp.einsum("qkgd,nkd->qkgn", query_part, flat_keys, preferred_element_type=jnp.float32)
        * query_scale
    )
    scores = softcap * jnp.tanh(scores / softcap)
    key_pid = jnp.repeat(jnp.arange(prefix_count, dtype=jnp.int32), row_count)
    key_pos = first + jnp.tile(jnp.arange(row_count, dtype=jnp.int32), prefix_count)
    matches = key_pid[:, None] == jnp.arange(prefix_count, dtype=jnp.int32)[None, :]
    length_cap = jnp.sum(jnp.where(matches, prefix_len[None, :], 0), 1)
    usable = (token_pid[:, None] == key_pid[None, :]) & (key_pos[None, :] < length_cap[None, :])
    weights = jnp.where(usable[:, None, None, :], jnp.exp(scores), jnp.float32(0.0))
    summed = jnp.einsum(
        "qkgn,nkd->qkgd",
        weights.astype(jnp.bfloat16),
        flat_vals,
        preferred_element_type=jnp.float32,
    )
    return (summed, jnp.sum(weights, -1))


def shards(
    hidden_in,
    queries,
    suffix_kv,
    prefix_kv,
    hyp_prefix,
    suffix_len,
    prefix_len,
    w_out,
    gain_attn,
    gain_pre,
    w_gate,
    w_up,
    w_down,
):
    n_ctx = lax.axis_size("ctx")
    ctx_index = lax.axis_index("ctx")
    req_index = lax.axis_index("req")
    tok_rows = queries.shape[0]
    hyp_count = hyp_prefix.shape[0]
    suffix_rows = tok_rows // hyp_count
    prefix_count = prefix_len.shape[0]
    head_group = HEADS // KV_HEADS
    kv_local = KV_HEADS // n_ctx
    width_local = kv_local * head_group * HEAD
    token_pid = jnp.repeat(hyp_prefix - req_index * prefix_count, suffix_rows)
    query_own = lax.dynamic_slice_in_dim(queries, ctx_index * width_local, width_local, 1).reshape(
        tok_rows, kv_local, head_group, HEAD
    )
    own_heads = lax.all_to_all(prefix_kv, "ctx", split_axis=3, concat_axis=2, tiled=True)
    whole = own_heads.shape[2]
    key_block = own_heads[0].reshape(prefix_count, whole, kv_local, HEAD)
    value_block = own_heads[1].reshape(prefix_count, whole, kv_local, HEAD)
    summed, total = prefix_terms(key_block, value_block, 0, query_own, token_pid, prefix_len)
    suffix_own = lax.dynamic_slice_in_dim(
        suffix_kv, ctx_index * kv_local * HEAD, kv_local * HEAD, 2
    )
    suf_keys = suffix_own[0].reshape(hyp_count, suffix_rows, kv_local, HEAD)
    suf_vals = suffix_own[1].reshape(hyp_count, suffix_rows, kv_local, HEAD)
    query_hyp = query_own.reshape(hyp_count, suffix_rows, kv_local, head_group, HEAD)
    scores = (
        jnp.einsum("hskgd,htkd->hskgt", query_hyp, suf_keys, preferred_element_type=jnp.float32)
        * query_scale
    )
    scores = softcap * jnp.tanh(scores / softcap)
    places = jnp.arange(suffix_rows, dtype=jnp.int32)
    usable = (places[None, None, :] <= places[None, :, None]) & (
        places[None, None, :] < suffix_len[:, None, None]
    )
    weights = jnp.where(usable[:, :, None, None, :], jnp.exp(scores), jnp.float32(0.0))
    suf_sum = jnp.einsum(
        "hskgt,htkd->hskgd",
        weights.astype(jnp.bfloat16),
        suf_vals,
        preferred_element_type=jnp.float32,
    )
    summed = summed + suf_sum.reshape(tok_rows, kv_local, head_group, HEAD)
    total = total + jnp.sum(weights, -1).reshape(tok_rows, kv_local, head_group)
    attn = (summed / total[..., None]).astype(jnp.bfloat16).reshape(tok_rows, width_local)
    proj = lax.psum(jnp.dot(attn, w_out, preferred_element_type=jnp.float32), "ctx")
    scale_a = lax.rsqrt(jnp.mean(proj * proj, -1, keepdims=True) + eps)
    resid = (hidden_in.astype(jnp.float32) + gain_attn * proj * scale_a).astype(jnp.bfloat16)
    resid_f = resid.astype(jnp.float32)
    scale_b = lax.rsqrt(jnp.mean(resid_f * resid_f, -1, keepdims=True) + eps)
    normed = (resid_f * scale_b * gain_pre).astype(jnp.bfloat16)
    piece = lax.all_gather(normed, "req", axis=0, tiled=True)
    gate = jnp.dot(piece, w_gate, preferred_element_type=jnp.float32)
    upper = jnp.dot(piece, w_up, preferred_element_type=jnp.float32)
    hidden = (jax.nn.gelu(gate, approximate=True) * upper).astype(jnp.bfloat16)
    partial_out = jnp.dot(
        lax.all_gather(hidden, "ctx", axis=1, tiled=True),
        w_down,
        preferred_element_type=jnp.float32,
    )
    ffn_out = lax.psum_scatter(partial_out, "req", scatter_dimension=0, tiled=True).astype(
        jnp.bfloat16
    )
    return (resid, ffn_out)


def solution(mesh):
    placed = (
        P("req", None),
        P("req", None),
        P(None, "req", None),
        P(None, "req", "ctx", None),
        P("req"),
        P("req"),
        P("req"),
        P("ctx", None),
        P(),
        P(),
        P(None, ("req", "ctx")),
        P(None, ("req", "ctx")),
        P("req", "ctx"),
    )
    return jax.shard_map(
        shards,
        mesh=mesh,
        in_specs=placed,
        out_specs=(P("req", None), P("req", "ctx")),
        check_vma=False,
    )
```

profile of v0, /device:TPU:1, one launch (start us, length us, event | category | flops | bytes accessed | tf_op | source)
XLA Modules:
  0.0 518.6 jit_solution(2958540260433920978)
XLA Ops:
  7.2 6.3 %copy.32 = bf16[2,2,128,2048]{2,1,0,3:T(2,128)(2,1)} copy(bf16[2,2,128,2048]{3,2,1,0:T(8,128)(2,1)} %param.16) | data formatting | bytes 4194304 | tf_op args[3]
  13.5 10.3 %all-to-all-start = ((bf16[2,2,128,2048]{2,1,0,3:T(2,128)(2,1)}), bf16[2,2,128,2048]{2,1,0,3:T(2,128)(2,1)}, u32[]{:S(2)}, u32[]{:S(2)}) async-start(bf16[2,2,128,2048]{2,1,0,3:T(2,128)(2,1)} %copy.32), calls=%async_computation | async-start | bytes 4194304 | tf_op jit(solution)/shard_map/all_to_all | solution.py:71
  23.9 0.1 broadcast_in_dim.58
  24.0 0.1 eq.36
  24.1 0.8 constant_dynamic-slice_fusion.1
  24.9 0.7 constant_dynamic-slice_fusion
  25.6 0.1 iota_compare_fusion.1
  25.7 0.1 broadcast_and_fusion
  25.8 0.2 fusion.37
  26.0 0.1 reshape.199
  26.1 0.2 convolution_bitcast_fusion
  26.3 0.1 fusion.26
  26.5 0.2 compare_and_fusion
  26.7 45.4 %all-to-all-done = bf16[2,2,128,2048]{2,1,0,3:T(2,128)(2,1)} async-done(((bf16[2,2,128,2048]{2,1,0,3:T(2,128)(2,1)}), bf16[2,2,128,2048]{2,1,0,3:T(2,128)(2,1)}, u32[]{:S(2)}, u32[]{:S(2)}) %all-to-all-start) | async-done | bytes 2097184 | tf_op jit(solution)/shard_map/all_to_all | solution.py:71
  72.1 6.1 %copy.33 = bf16[2,2,128,16,128]{4,2,3,1,0:T(8,128)(2,1)} copy(bf16[2,2,128,16,128]{2,1,0,4,3:T(2,128)(2,1)} %bitcast) | data formatting | bytes 4194304 | tf_op jit(solution)/shard_map/all_to_all | solution.py:71
  78.3 1.7 fusion.35
  80.0 1.7 fusion.36
  81.7 0.5 fusion.15
  82.2 1.6 fusion.27
  83.8 131.1 %all-reduce.2.cloned.1.call-done = f32[64,4608]{1,0:T(8,128)} async-done(((f32[64,4608]{1,0:T(8,128)}), f32[64,4608]{1,0:T(8,128)}) %all-reduce.2.cloned.1.call-update) | async-done | bytes 1179664 | tf_op jit(solution)/shard_map/psum | solution.py:101
  214.9 1.5 multiply_reduce_fusion
  216.5 0.1 copy-done.1
  216.5 1.1 fusion.6
  217.7 1.0 fusion.8
  218.8 0.0 all-gather.5.cloned.1.call-start
  218.8 91.8 %all-gather.3.cloned.1.call-done = bf16[1024,4608]{1,0:T(8,128)(2,1)} async-done(((bf16[64,4608]{1,0:T(8,128)(2,1)}), bf16[1024,4608]{1,0:T(8,128)(2,1)}) %all-gather.3.cloned.1.call-update) | async-done | bytes 9437200 | tf_op jit(solution)/shard_map/all_gather | solution.py:107
  310.6 7.3 %fusion.38 = f32[1024,144]{0,1:T(8,128)S(1)} fusion(bf16[1024,4608]{1,0:T(8,128)(2,1)} %all-gather.3.cloned.1.call-done, bf16[4608,144]{0,1:T(8,128)(2,1)} %param.23), kind=kOutput, calls=%fused_computation.61 | convolution fusion | flops 1358954496 | bytes 11354112 | tf_op jit(solution)/shard_map/dot_general | solution.py:108
  318.0 3.9 fusion.5
  322.0 105.8 %all-gather.5.cloned.1.call-done = bf16[1024,2304]{0,1:T(8,128)(2,1)} async-done(((bf16[1024,144]{0,1:T(8,128)(2,1)}), bf16[1024,2304]{0,1:T(8,128)(2,1)}) %all-gather.5.cloned.1.call-update) | async-done | bytes 4718608 | tf_op jit(solution)/shard_map/all_gather | solution.py:112
  427.8 6.6 %fusion.39 = f32[1024,288]{1,0:T(8,128)} fusion(bf16[1024,2304]{0,1:T(8,128)(2,1)} %all-gather.5.cloned.1.call-done, bf16[2304,288]{0,1:T(8,128)(2,1)} %param.25), kind=kOutput, calls=%fused_computation.62 | convolution fusion | flops 1358954496 | bytes 7225344 | tf_op jit(solution)/shard_map/dot_general | solution.py:111
  434.4 76.1 %reduce-scatter.2.cloned.1.call-done = f32[64,288]{1,0:T(8,128)} async-done(((f32[1024,288]{1,0:T(8,128)}), f32[64,288]{1,0:T(8,128)}) %reduce-scatter.2.cloned.1.call-update) | async-done | bytes 73744 | tf_op jit(solution)/shard_map/reduce_scatter | solution.py:116
  510.5 1.5 convert_element_type.35
  (40 shorter events, 0.4 us)
Async XLA Ops:
  7.2 75.0 %copy-start = (bf16[256,4608]{1,0:T(8,128)(2,1)S(1)}, bf16[256,4608]{1,0:T(8,128)(2,1)}, u32[]{:S(2)}) copy-start(bf16[256,4608]{1,0:T(8,128)(2,1)} %param.20) | copy-start | bytes 7077892
  13.5 10.4 %copy-start.8 = (s32[4]{0:T(128)S(1)}, s32[4]{0:T(128)}, u32[]{:S(2)}) copy-start(s32[4]{0:T(128)} %param.17) | copy-start | bytes 52
  13.5 12.2 %copy-start.9 = (s32[4]{0:T(128)S(1)}, s32[4]{0:T(128)}, u32[]{:S(2)}) copy-start(s32[4]{0:T(128)} %param.18) | copy-start | bytes 52
  13.5 12.8 %copy-start.5 = (s32[2]{0:T(128)S(1)}, s32[2]{0:T(128)}, u32[]{:S(2)}) copy-start(s32[2]{0:T(128)} %param.19) | copy-start | bytes 28
  13.5 58.6 %all-to-all-start = ((bf16[2,2,128,2048]{2,1,0,3:T(2,128)(2,1)}), bf16[2,2,128,2048]{2,1,0,3:T(2,128)(2,1)}, u32[]{:S(2)}, u32[]{:S(2)}) async-start(bf16[2,2,128,2048]{2,1,0,3:T(2,128)(2,1)} %copy.32), calls=%async_computation | async-start | bytes 4194304 | tf_op jit(solution)/shard_map/all_to_all | solution.py:71
  23.8 191.1 %all-reduce.2.cloned.1.call-start = ((), (), s32[]{:S(2)}) async-start(), calls=%async_computation.2 | async-start | bytes 2359296 | tf_op jit(solution)/shard_map/psum | solution.py:101
  83.8 132.7 %copy-start.3 = (bf16[64,4608]{1,0:T(8,128)(2,1)S(1)}, bf16[64,4608]{1,0:T(8,128)(2,1)}, u32[]{:S(2)}) copy-start(bf16[64,4608]{1,0:T(8,128)(2,1)} %param.13) | copy-start | bytes 1769476
  83.8 226.8 %all-gather.3.cloned.1.call-start = ((), (), s32[]{:S(2)}) async-start(), calls=%async_computation.3 | async-start | bytes 10027008 | tf_op jit(solution)/shard_map/all_gather | solution.py:107
  214.9 1.6 copy-start.1
  214.9 2.8 copy-start.4
  217.7 100.3 %copy-start.2 = (bf16[64,4608]{1,0:T(8,128)(2,1)}, bf16[64,4608]{1,0:T(8,128)(2,1)S(1)}, u32[]{:S(2)}) copy-start(bf16[64,4608]{1,0:T(8,128)(2,1)S(1)} %get-tuple-element.3) | copy-start | bytes 1769476
  218.8 209.0 %all-gather.5.cloned.1.call-start = ((), (), s32[]{:S(2)}) async-start(), calls=%async_computation.4 | async-start | bytes 5013504 | tf_op jit(solution)/shard_map/all_gather | solution.py:112
  310.6 7.3 %copy-start.6 = (bf16[1024,4608]{1,0:T(8,128)(2,1)S(1)}, bf16[1024,4608]{1,0:T(8,128)(2,1)}, u32[]{:S(2)}) copy-start(bf16[1024,4608]{1,0:T(8,128)(2,1)} %all-gather.3.cloned.1.call-done) | copy-start | bytes 28311556
  310.6 7.4 %copy-start.7 = (bf16[4608,144]{0,1:T(8,128)(2,1)S(1)}, bf16[4608,144]{0,1:T(8,128)(2,1)}, u32[]{:S(2)}) copy-start(bf16[4608,144]{0,1:T(8,128)(2,1)} %param.24) | copy-start | bytes 3981316
  321.9 188.6 %reduce-scatter.2.cloned.1.call-start = ((), (), s32[]{:S(2)}) async-start(), calls=%async_computation.5 | async-start | bytes 1671168 | tf_op jit(solution)/shard_map/reduce_scatter | solution.py:116
Sparse Core Ops, SparseCore 0:
  83.9 130.9 all-reduce.1
  218.9 91.6 all-gather.2
  322.0 105.7 all-gather.4
  434.5 75.9 reduce-scatter.1
where the time goes:
time: 520 us; the launch traced here: 519 us
  waiting for transfers between devices  450 us (87%)
  matrix products  21.9 us (4%)
  local copies, waits for them, and re-layouts  16.1 us (3%)
  between operations  14 us (3%)
  starting transfers between devices  10.5 us (2%)
  other arithmetic  5.78 us (1%)
    psum x1, waiting for transfers between devices, shards(): lax.psum(jnp.dot(attn, w_out, preferred_element_type=jnp.float32), 'ctx')  131 us
    all_gather x1, waiting for transfers between devices, shards(): lax.all_gather(hidden, 'ctx', axis=1, tiled=True)  106 us
    all_gather x1, waiting for transfers between devices, shards(): piece = lax.all_gather(normed, 'req', axis=0, tiled=True)  91.8 us
    reduce_scatter x1, waiting for transfers between devices, shards(): lax.psum_scatter(partial_out, 'req', scatter_dimension=0, tiled=True)  76.1 us
    all_to_all x1, waiting for transfers between devices, shards(): lax.all_to_all(prefix_kv, 'ctx', split_axis=3, concat_axis=2, tiled=True)  45.4 us
  transfers between devices with their start and end apart: 5, of which 5 were waited for; matrix products, arithmetic and copies ran while one was open for 1% of the time, Pallas kernels for 0%

commit v1 on v0

v1 whole, which is shorter than its diff:
```python
import functools

import jax
import jax.numpy as jnp
from jax import lax
from jax.experimental import pallas as pl
from jax.experimental.pallas import tpu as pltpu
from jax.sharding import PartitionSpec as P

HEADS = 32
KV_HEADS = 16
HEAD = 128

softcap = 50.0
query_scale = 144.0 ** (-0.5)
eps = 1e-06

NT = (((1,), (1,)), ((), ()))
NN = (((1,), (0,)), ((), ()))


def weights_of(scores):
    return jnp.exp(softcap * jnp.tanh(scores * (query_scale / softcap)))


def attention_kernel(
    n,
    queries,
    suffix_kv,
    prefix_kv,
    hyp_prefix,
    suffix_len,
    prefix_len,
    w_out,
    hidden_in,
    gain_attn,
    resid_out,
    mask,
    part_send,
    part_recv,
    proj_send,
    proj_recv,
    part_ssem,
    part_rsem,
    proj_ssem,
    proj_rsem,
    resid_ssem,
    resid_rsem,
):
    me = lax.axis_index("ctx")
    req = lax.axis_index("req")
    tokens = queries.shape[0]
    prefixes, block = prefix_kv.shape[1], prefix_kv.shape[2]
    group = HEADS // KV_HEADS
    rows = group * tokens
    hyps = hyp_prefix.shape[0]
    suf = tokens // hyps
    slab = tokens // n
    width = w_out.shape[1]

    barrier = pltpu.get_barrier_semaphore()

    def greet(s, _):
        pl.semaphore_signal(
            barrier, inc=1, device_id={"ctx": lax.rem(me + s, n)}, device_id_type=pl.DeviceIdType.MESH
        )
        return 0

    lax.fori_loop(1, n, greet, 0)

    row = lax.broadcasted_iota(jnp.int32, (rows, prefixes * block), 0)
    col = lax.broadcasted_iota(jnp.int32, (rows, prefixes * block), 1)
    hyp_of_row = lax.rem(row, tokens) // suf
    row_pid = jnp.zeros_like(row)
    for h in range(hyps):
        row_pid = jnp.where(hyp_of_row == h, hyp_prefix[h] - req * prefixes, row_pid)
    col_pid = col // block
    col_len = jnp.zeros_like(row)
    for p in range(prefixes):
        col_len = jnp.where(col_pid == p, prefix_len[p], col_len)
    ok = (row_pid == col_pid) & (me * block + lax.rem(col, block) < col_len)
    mask[...] = jnp.where(ok, 1.0, 0.0)
    eye = lax.broadcasted_iota(jnp.int32, (rows, rows), 0) == lax.broadcasted_iota(jnp.int32, (rows, rows), 1)

    pl.semaphore_wait(barrier, n - 1)

    def query_rows(head):
        both = queries[:, pl.ds(pl.multiple_of(head * (group * HEAD), group * HEAD), group * HEAD)]
        return jnp.concatenate([both[:, g * HEAD : (g + 1) * HEAD] for g in range(group)], 0)

    def partial_of(head):
        lanes = pl.ds(pl.multiple_of(head * HEAD, HEAD), HEAD)
        query = query_rows(head)
        keys = prefix_kv[0, :, :, lanes].reshape(prefixes * block, HEAD)
        vals = prefix_kv[1, :, :, lanes].reshape(prefixes * block, HEAD)
        scores = lax.dot_general(query, keys, NT, preferred_element_type=jnp.float32)
        weights = jnp.where(mask[...] > 0.5, weights_of(scores), 0.0)
        summed = jnp.dot(weights.astype(jnp.bfloat16), vals, preferred_element_type=jnp.float32)
        return summed, jnp.sum(weights, 1, keepdims=True)

    def store_partial(ref, summed, total):
        ref[0:rows, :] = summed.astype(jnp.bfloat16)
        flat = jnp.sum(jnp.where(eye, total, 0.0), 0, keepdims=True)
        high = flat.astype(jnp.bfloat16).astype(jnp.float32)
        low = flat - high
        place = lax.broadcasted_iota(jnp.int32, (16, rows), 0)
        ref[rows : rows + 16, :] = jnp.where(
            place == 0, high, jnp.where(place == 1, low, 0.0)
        ).astype(jnp.bfloat16)

    def part_copy(peer):
        return pltpu.make_async_remote_copy(
            src_ref=part_send.at[peer],
            dst_ref=part_recv.at[me],
            send_sem=part_ssem.at[peer],
            recv_sem=part_rsem.at[me],
            device_id={"ctx": peer},
            device_id_type=pl.DeviceIdType.MESH,
        )

    def send_part(s, _):
        peer = lax.rem(me + s, n)
        summed, total = partial_of(peer)
        store_partial(part_send.at[peer], summed, total)
        part_copy(peer).start()
        return 0

    lax.fori_loop(1, n, send_part, 0, unroll=3)

    summed, total = partial_of(me)
    own = pl.ds(pl.multiple_of(me * HEAD, HEAD), HEAD)
    suf_row = lax.rem(lax.broadcasted_iota(jnp.int32, (rows, tokens), 0), tokens)
    suf_col = lax.broadcasted_iota(jnp.int32, (rows, tokens), 1)
    row_hyp, col_hyp = suf_row // suf, suf_col // suf
    place = suf_col - col_hyp * suf
    length = jnp.zeros_like(suf_row)
    for h in range(hyps):
        length = jnp.where(col_hyp == h, suffix_len[h], length)
    usable = (row_hyp == col_hyp) & (suf_col <= suf_row) & (place < length)
    scores = lax.dot_general(query_rows(me), suffix_kv[0, :, own], NT, preferred_element_type=jnp.float32)
    weights = jnp.where(usable, weights_of(scores), 0.0)
    summed += jnp.dot(weights.astype(jnp.bfloat16), suffix_kv[1, :, own], preferred_element_type=jnp.float32)
    total += jnp.sum(weights, 1, keepdims=True)

    def add_part(s, carry):
        summed, flat = carry
        peer = lax.rem(me + n - s, n)
        part = part_recv.at[peer]
        pltpu.make_async_remote_copy(
            src_ref=part_send.at[peer],
            dst_ref=part,
            send_sem=part_ssem.at[peer],
            recv_sem=part_rsem.at[peer],
            device_id={"ctx": peer},
            device_id_type=pl.DeviceIdType.MESH,
        ).wait_recv()
        summed = summed + part[0:rows, :].astype(jnp.float32)
        flat = flat + part[rows : rows + 16, :].astype(jnp.float32)
        return summed, flat

    summed, flat = lax.fori_loop(1, n, add_part, (summed, jnp.zeros((16, rows), jnp.float32)))
    flat = jnp.sum(flat, 0, keepdims=True)
    total += jnp.sum(jnp.where(eye, flat, 0.0), 1, keepdims=True)
    attn = (summed / total).astype(jnp.bfloat16)
    attn = jnp.concatenate([attn[g * tokens : (g + 1) * tokens] for g in range(group)], 1)

    step = 512
    for c in range(0, width, step):
        term = jnp.dot(attn, w_out[:, c : c + step], preferred_element_type=jnp.float32)
        for i in range(n):
            proj_send[i, :, c : c + step] = term[i * slab : (i + 1) * slab].astype(jnp.bfloat16)

    def proj_copy(peer, slot):
        return pltpu.make_async_remote_copy(
            src_ref=proj_send.at[peer],
            dst_ref=proj_recv.at[slot],
            send_sem=proj_ssem.at[peer],
            recv_sem=proj_rsem.at[slot],
            device_id={"ctx": peer},
            device_id_type=pl.DeviceIdType.MESH,
        )

    def send_proj(s, _):
        proj_copy(lax.rem(me + s, n), me).start()
        return 0

    lax.fori_loop(1, n, send_proj, 0)

    around = hidden_in[pl.ds(pl.multiple_of(me * slab // 16 * 16, 16), 16), :].astype(jnp.float32)
    mine = jnp.zeros((slab, width), jnp.float32)
    for g in range(16 // slab):
        mine = jnp.where(lax.rem(me, 16 // slab) == g, around[g * slab : (g + 1) * slab], mine)

    def add_proj(s, proj):
        peer = lax.rem(me + n - s, n)
        proj_copy(peer, peer).wait_recv()
        return proj + proj_recv[peer].astype(jnp.float32)

    proj = lax.fori_loop(1, n, add_proj, proj_send[me].astype(jnp.float32))
    scale_a = lax.rsqrt(jnp.mean(proj * proj, 1, keepdims=True) + eps)
    resid_out[me] = (mine + gain_attn[...] * proj * scale_a).astype(jnp.bfloat16)

    def resid_copy(peer, slot):
        return pltpu.make_async_remote_copy(
            src_ref=resid_out.at[slot],
            dst_ref=resid_out.at[slot],
            send_sem=resid_ssem.at[peer],
            recv_sem=resid_rsem.at[slot],
            device_id={"ctx": peer},
            device_id_type=pl.DeviceIdType.MESH,
        )

    def send_resid(s, _):
        resid_copy(lax.rem(me + s, n), me).start()
        return 0

    lax.fori_loop(1, n, send_resid, 0)

    def finish(s, _):
        peer = lax.rem(me + s, n)
        resid_copy(peer, peer).wait_recv()
        part_copy(peer).wait_send()
        proj_copy(peer, me).wait_send()
        resid_copy(peer, me).wait_send()
        return 0

    lax.fori_loop(1, n, finish, 0)


def attention(n, queries, suffix_kv, prefix_kv, hyp_prefix, suffix_len, prefix_len, w_out, hidden_in, gain_attn):
    tokens, width = hidden_in.shape
    rows = HEADS // KV_HEADS * tokens
    slab = tokens // n
    positions = prefix_kv.shape[1] * prefix_kv.shape[2]
    vmem = pl.BlockSpec(memory_space=pltpu.VMEM)
    smem = pl.BlockSpec(memory_space=pltpu.SMEM)
    dma = pltpu.SemaphoreType.DMA((n,))
    resid = pl.pallas_call(
        functools.partial(attention_kernel, n),
        out_shape=jax.ShapeDtypeStruct((n, slab, width), jnp.bfloat16),
        in_specs=[vmem, vmem, vmem, smem, smem, smem, vmem, vmem, vmem],
        out_specs=vmem,
        scratch_shapes=[
            pltpu.VMEM((rows, positions), jnp.float32),
            pltpu.VMEM((n, rows + 16, HEAD), jnp.bfloat16),
            pltpu.VMEM((n, rows + 16, HEAD), jnp.bfloat16),
            pltpu.VMEM((n, slab, width), jnp.bfloat16),
            pltpu.VMEM((n, slab, width), jnp.bfloat16),
            dma,
            dma,
            dma,
            dma,
            dma,
            dma,
        ],
        compiler_params=pltpu.CompilerParams(
            collective_id=0, has_side_effects=True, vmem_limit_bytes=40 * 2**20
        ),
        cost_estimate=pl.CostEstimate(flops=10**9, bytes_accessed=10**7, transcendentals=10**6),
        name="attention_projection",
    )(queries, suffix_kv, prefix_kv, hyp_prefix, suffix_len, prefix_len, w_out, hidden_in, gain_attn.reshape(1, -1))
    return resid.reshape(tokens, width)


def shards(
    hidden_in,
    queries,
    suffix_kv,
    prefix_kv,
    hyp_prefix,
    suffix_len,
    prefix_len,
    w_out,
    gain_attn,
    gain_pre,
    w_gate,
    w_up,
    w_down,
):
    n_ctx = lax.axis_size("ctx")
    resid = attention(
        n_ctx, queries, suffix_kv, prefix_kv, hyp_prefix, suffix_len, prefix_len, w_out, hidden_in, gain_attn
    )
    resid_f = resid.astype(jnp.float32)
    scale_b = lax.rsqrt(jnp.mean(resid_f * resid_f, -1, keepdims=True) + eps)
    normed = (resid_f * scale_b * gain_pre).astype(jnp.bfloat16)
    piece = lax.all_gather(normed, "req", axis=0, tiled=True)
    gate = jnp.dot(piece, w_gate, preferred_element_type=jnp.float32)
    upper = jnp.dot(piece, w_up, preferred_element_type=jnp.float32)
    hidden = (jax.nn.gelu(gate, approximate=True) * upper).astype(jnp.bfloat16)
    partial_out = jnp.dot(
        lax.all_gather(hidden, "ctx", axis=1, tiled=True),
        w_down,
        preferred_element_type=jnp.float32,
    )
    ffn_out = lax.psum_scatter(partial_out, "req", scatter_dimension=0, tiled=True).astype(
        jnp.bfloat16
    )
    return (resid, ffn_out)


def solution(mesh):
    placed = (
        P("req", None),
        P("req", None),
        P(None, "req", None),
        P(None, "req", "ctx", None),
        P("req"),
        P("req"),
        P("req"),
        P("ctx", None),
        P(),
        P(),
        P(None, ("req", "ctx")),
        P(None, ("req", "ctx")),
        P("req", "ctx"),
    )
    return jax.shard_map(
        shards,
        mesh=mesh,
        in_specs=placed,
        out_specs=(P("req", None), P("req", "ctx")),
        check_vma=False,
    )
```

time: 520 us -> 368 us (0.71)
  waiting for transfers between devices: 450 us -> 268 us
  Pallas kernels: 0 us -> 55.3 us
  starting transfers between devices: 10.5 us -> 0.12 us
  local copies, waits for them, and re-layouts: 16.1 us -> 9.51 us
    psum x1 -> x0, waiting for transfers between devices: 131 us -> none  [shards(): lax.psum(jnp.dot(attn, w_out, preferred_element_type=jnp.float32), 'ctx')]
    pallas_call x0 -> x1, Pallas kernels: none -> 55.3 us  [attention(): pl.pallas_call(functools.partial(attention_kernel, n), out_shape=jax.Shap...]
    all_to_all x1 -> x0, waiting for transfers between devices: 45.4 us -> none  [shards(): lax.all_to_all(prefix_kv, 'ctx', split_axis=3, concat_axis=2, tiled=True)]
    all_to_all x1 -> x0, starting transfers between devices: 10.3 us -> none  [shards(): lax.all_to_all(prefix_kv, 'ctx', split_axis=3, concat_axis=2, tiled=True)]
    all_to_all x1 -> x0, local copies, waits for them, and re-layouts: 6.15 us -> none  [shards(): lax.all_to_all(prefix_kv, 'ctx', split_axis=3, concat_axis=2, tiled=True)]
    all_gather x1, waiting for transfers between devices: 91.8 us -> 86.3 us  [shards(): piece = lax.all_gather(normed, 'req', axis=0, tiled=True)]
  transfers between devices with their start and end apart: 5 -> 3, of which waited for: 5 -> 3; matrix products, arithmetic and copies ran while one was open for 1% -> 0% of each run, Pallas kernels for 0% -> 0%
where the time goes in v1:
time: 368 us; the launch traced here: 367 us
  waiting for transfers between devices  268 us (73%)
  Pallas kernels  55.3 us (15%)
  matrix products  17.1 us (5%)
  between operations  13.9 us (4%)
  local copies, waits for them, and re-layouts  9.51 us (3%)
    all_gather x1, waiting for transfers between devices, shards(): lax.all_gather(hidden, 'ctx', axis=1, tiled=True)  106 us
    all_gather x1, waiting for transfers between devices, shards(): piece = lax.all_gather(normed, 'req', axis=0, tiled=True)  86.3 us
    reduce_scatter x1, waiting for transfers between devices, shards(): lax.psum_scatter(partial_out, 'req', scatter_dimension=0, tiled=True)  76.2 us
    pallas_call x1, Pallas kernels, attention(): pl.pallas_call(functools.partial(attention_kernel, n), out_shape=jax.Shap...  55.3 us
    unnamed x28, local copies, waits for them, and re-layouts  8.46 us
  transfers between devices with their start and end apart: 3, of which 3 were waited for; matrix products, arithmetic and copies ran while one was open for 0% of the time, Pallas kernels for 0%

profile of v1, /device:TPU:1, one launch (start us, length us, event | category | flops | bytes accessed | tf_op | source)
XLA Modules:
  0.0 367.1 jit_solution(9777131289948024514)
XLA Ops:
  7.2 0.0 copy-start
  7.2 0.0 all-gather.3.cloned.1.call-start
  7.2 0.8 reshape.28.gain_attn
  8.1 0.0 copy-start.1
  8.1 1.7 copy-done.1
  9.7 1.6 copy-done.2
  11.3 1.1 copy-done.3
  12.4 1.0 copy-done.4
  13.4 1.0 copy-done.5
  14.5 0.7 copy-done.6
  15.1 0.7 copy-done.7
  15.8 0.7 copy-done.8
  16.4 55.3 %attention_projection.1 = bf16[16,4,4608]{2,1,0:T(4,128)(2,1)S(1)} custom-call(bf16[64,4096]{1,0:T(8,128)(2,1)S(1)} %copy-done.4, bf16[2,64,2048]{2,1,0:T(8,128)(2,1)S(1)} %copy-done.5, bf16[2,2,128,2048]{3,2,1,0:T(8,128)(2,1)S(1)} %copy-done.2, s32[4]{0:T(128)S(1)} %copy-done.6, s32[4]{0:T(128)S(1)} %copy-done.7, s32[2]{0:T(128)S(1)} %copy-done.8, ...), custom_call_target="tpu_custom_call" | custom-call | flops 1000000000 | bytes 10000000 | tf_op jit(solution)/shard_map/attention_projection/pallas_call | solution.py:238
  71.7 0.0 copy-start.10
  71.7 0.4 multiply_reduce_fusion
  72.1 0.1 reshape.29
  72.3 0.0 copy-start.9
  72.3 0.1 rsqrt.12
  72.4 0.1 copy-done.10
  72.4 1.0 multiply_convert_fusion
  73.5 0.0 all-gather.3.cloned.1.call-update
  73.5 0.0 all-gather.5.cloned.1.call-start
  73.5 86.3 %all-gather.3.cloned.1.call-done = bf16[1024,4608]{1,0:T(8,128)(2,1)} async-done(((bf16[64,4608]{1,0:T(8,128)(2,1)}), bf16[1024,4608]{1,0:T(8,128)(2,1)}) %all-gather.3.cloned.1.call-update) | async-done | bytes 9437200 | tf_op jit(solution)/shard_map/all_gather | solution.py:287
  159.8 7.0 %fusion.8 = f32[1024,144]{0,1:T(8,128)S(1)} fusion(bf16[1024,4608]{1,0:T(8,128)(2,1)} %all-gather.3.cloned.1.call-done, bf16[4608,144]{0,1:T(8,128)(2,1)S(1)} %copy-done.12), kind=kOutput, calls=%fused_computation.13 | convolution fusion | flops 1358954496 | bytes 11354112 | tf_op jit(solution)/shard_map/dot_general | solution.py:288
  166.8 3.9 %fusion = bf16[1024,144]{0,1:T(8,128)(2,1)} fusion(bf16[1024,4608]{1,0:T(8,128)(2,1)S(1)} %copy-done.11, bf16[4608,144]{0,1:T(8,128)(2,1)S(1)} %copy-done.13, f32[1024,144]{0,1:T(8,128)S(1)} %fusion.8), kind=kOutput, calls=%fused_computation.1 | convolution fusion | flops 1360429056 | bytes 11649024 | tf_op jit(solution)/shard_map/dot_general | solution.py:289
  170.7 0.0 all-gather.5.cloned.1.call-update
  170.8 0.0 reduce-scatter.2.cloned.1.call-start
  170.8 105.8 %all-gather.5.cloned.1.call-done = bf16[1024,2304]{0,1:T(8,128)(2,1)} async-done(((bf16[1024,144]{0,1:T(8,128)(2,1)}), bf16[1024,2304]{0,1:T(8,128)(2,1)}) %all-gather.5.cloned.1.call-update) | async-done | bytes 4718608 | tf_op jit(solution)/shard_map/all_gather | solution.py:292
  276.7 6.2 %fusion.9 = f32[1024,288]{1,0:T(8,128)} fusion(bf16[1024,2304]{0,1:T(8,128)(2,1)} %all-gather.5.cloned.1.call-done, bf16[2304,288]{0,1:T(8,128)(2,1)S(1)} %copy-done), kind=kOutput, calls=%fused_computation.14 | convolution fusion | flops 1358954496 | bytes 7225344 | tf_op jit(solution)/shard_map/dot_general | solution.py:291
  282.8 0.0 reduce-scatter.2.cloned.1.call-update
  282.9 76.2 %reduce-scatter.2.cloned.1.call-done = f32[64,288]{1,0:T(8,128)} async-done(((f32[1024,288]{1,0:T(8,128)}), f32[64,288]{1,0:T(8,128)}) %reduce-scatter.2.cloned.1.call-update) | async-done | bytes 73744 | tf_op jit(solution)/shard_map/reduce_scatter | solution.py:296
  359.0 1.5 convert_element_type.19
  (16 shorter events, 0.0 us)
Async XLA Ops:
  7.2 269.5 %copy-start = (bf16[2304,288]{0,1:T(8,128)(2,1)S(1)}, bf16[2304,288]{0,1:T(8,128)(2,1)}, u32[]{:S(2)}) copy-start(bf16[2304,288]{0,1:T(8,128)(2,1)} %param.25) | copy-start | bytes 3981316
  7.2 152.6 %all-gather.3.cloned.1.call-start = ((), (), s32[]{:S(2)}) async-start(), calls=%async_computation.1 | async-start | bytes 10027008 | tf_op jit(solution)/shard_map/all_gather | solution.py:287
  8.1 1.7 copy-start.1
  9.7 1.6 copy-start.2
  11.3 1.1 copy-start.3
  12.4 1.0 copy-start.4
  13.4 1.0 copy-start.5
  14.5 0.7 copy-start.6
  15.1 0.7 copy-start.7
  15.8 0.7 copy-start.8
  71.7 0.7 copy-start.10
  72.3 94.5 %copy-start.9 = (bf16[64,4608]{1,0:T(8,128)(2,1)}, bf16[64,4608]{1,0:T(8,128)(2,1)S(1)}, u32[]{:S(2)}) copy-start(bf16[64,4608]{1,0:T(8,128)(2,1)S(1)} %reshape.29) | copy-start | bytes 1769476
  72.3 87.5 %copy-start.12 = (bf16[4608,144]{0,1:T(8,128)(2,1)S(1)}, bf16[4608,144]{0,1:T(8,128)(2,1)}, u32[]{:S(2)}) copy-start(bf16[4608,144]{0,1:T(8,128)(2,1)} %param.23) | copy-start | bytes 3981316
  73.5 203.2 %all-gather.5.cloned.1.call-start = ((), (), s32[]{:S(2)}) async-start(), calls=%async_computation.2 | async-start | bytes 5013504 | tf_op jit(solution)/shard_map/all_gather | solution.py:292
  159.8 7.0 %copy-start.11 = (bf16[1024,4608]{1,0:T(8,128)(2,1)S(1)}, bf16[1024,4608]{1,0:T(8,128)(2,1)}, u32[]{:S(2)}) copy-start(bf16[1024,4608]{1,0:T(8,128)(2,1)} %all-gather.3.cloned.1.call-done) | copy-start | bytes 28311556
  159.8 7.0 %copy-start.13 = (bf16[4608,144]{0,1:T(8,128)(2,1)S(1)}, bf16[4608,144]{0,1:T(8,128)(2,1)}, u32[]{:S(2)}) copy-start(bf16[4608,144]{0,1:T(8,128)(2,1)} %param.24) | copy-start | bytes 3981316
  170.8 188.3 %reduce-scatter.2.cloned.1.call-start = ((), (), s32[]{:S(2)}) async-start(), calls=%async_computation.3 | async-start | bytes 1671168 | tf_op jit(solution)/shard_map/reduce_scatter | solution.py:296
Sparse Core Ops, SparseCore 0:
  73.6 86.1 all-gather.2
  170.9 105.7 all-gather.4
  283.0 75.9 reduce-scatter.1

commit v2 on v1

--- a/solution.py
+++ b/solution.py
@@ -17,6 +17,10 @@
 
 NT = (((1,), (1,)), ((), ()))
 NN = (((1,), (0,)), ((), ()))
+
+
+def slab_of(ctx):
+    return lax.rem(ctx, 2) * 8 + ctx // 2
 
 
 def weights_of(scores):
@@ -34,7 +38,9 @@
     w_out,
     hidden_in,
     gain_attn,
+    gain_pre,
     resid_out,
+    normed_out,
     mask,
     part_send,
     part_recv,
@@ -172,7 +178,7 @@
 
     def proj_copy(peer, slot):
         return pltpu.make_async_remote_copy(
-            src_ref=proj_send.at[peer],
+            src_ref=proj_send.at[slab_of(peer)],
             dst_ref=proj_recv.at[slot],
             send_sem=proj_ssem.at[peer],
             recv_sem=proj_rsem.at[slot],
@@ -186,21 +192,29 @@
 
     lax.fori_loop(1, n, send_proj, 0)
 
-    around = hidden_in[pl.ds(pl.multiple_of(me * slab // 16 * 16, 16), 16), :].astype(jnp.float32)
+    place = slab_of(me)
+    around = hidden_in[pl.ds(pl.multiple_of(place * slab // 16 * 16, 16), 16), :].astype(jnp.float32)
     mine = jnp.zeros((slab, width), jnp.float32)
     for g in range(16 // slab):
-        mine = jnp.where(lax.rem(me, 16 // slab) == g, around[g * slab : (g + 1) * slab], mine)
+        mine = jnp.where(lax.rem(place, 16 // slab) == g, around[g * slab : (g + 1) * slab], mine)
 
     def add_proj(s, proj):
         peer = lax.rem(me + n - s, n)
         proj_copy(peer, peer).wait_recv()
         return proj + proj_recv[peer].astype(jnp.float32)
 
-    proj = lax.fori_loop(1, n, add_proj, proj_send[me].astype(jnp.float32))
+    proj = lax.fori_loop(1, n, add_proj, proj_send[place].astype(jnp.float32))
     scale_a = lax.rsqrt(jnp.mean(proj * proj, 1, keepdims=True) + eps)
-    resid_out[me] = (mine + gain_attn[...] * proj * scale_a).astype(jnp.bfloat16)
+    resid = (mine + gain_attn[...] * proj * scale_a).astype(jnp.bfloat16)
+    resid_out[place] = resid
+    resid = resid.astype(jnp.float32)
+    scale_b = lax.rsqrt(jnp.mean(resid * resid, 1, keepdims=True) + eps)
+    normed = (resid * scale_b * gain_pre[...]).astype(jnp.bfloat16)
+    for half in range(2):
+        normed_out[half] = normed[:, half * (width // 2) : (half + 1) * (width // 2)]
 
     def resid_copy(peer, slot):
+        slot = slab_of(slot)
         return pltpu.make_async_remote_copy(
             src_ref=resid_out.at[slot],
             dst_ref=resid_out.at[slot],
@@ -227,7 +241,7 @@
     lax.fori_loop(1, n, finish, 0)
 
 
-def attention(n, queries, suffix_kv, prefix_kv, hyp_prefix, suffix_len, prefix_len, w_out, hidden_in, gain_attn):
+def attention(n, queries, suffix_kv, prefix_kv, hyp_prefix, suffix_len, prefix_len, w_out, hidden_in, gain_attn, gain_pre):
     tokens, width = hidden_in.shape
     rows = HEADS // KV_HEADS * tokens
     slab = tokens // n
@@ -235,11 +249,14 @@
     vmem = pl.BlockSpec(memory_space=pltpu.VMEM)
     smem = pl.BlockSpec(memory_space=pltpu.SMEM)
     dma = pltpu.SemaphoreType.DMA((n,))
-    resid = pl.pallas_call(
+    resid, normed = pl.pallas_call(
         functools.partial(attention_kernel, n),
-        out_shape=jax.ShapeDtypeStruct((n, slab, width), jnp.bfloat16),
-        in_specs=[vmem, vmem, vmem, smem, smem, smem, vmem, vmem, vmem],
-        out_specs=vmem,
+        out_shape=(
+            jax.ShapeDtypeStruct((n, slab, width), jnp.bfloat16),
+            jax.ShapeDtypeStruct((2, slab, width // 2), jnp.bfloat16),
+        ),
+        in_specs=[vmem, vmem, vmem, smem, smem, smem, vmem, vmem, vmem, vmem],
+        out_specs=(vmem, vmem),
         scratch_shapes=[
             pltpu.VMEM((rows, positions), jnp.float32),
             pltpu.VMEM((n, rows + 16, HEAD), jnp.bfloat16),
@@ -258,8 +275,440 @@
         ),
         cost_estimate=pl.CostEstimate(flops=10**9, bytes_accessed=10**7, transcendentals=10**6),
         name="attention_projection",
-    )(queries, suffix_kv, prefix_kv, hyp_prefix, suffix_len, prefix_len, w_out, hidden_in, gain_attn.reshape(1, -1))
-    return resid.reshape(tokens, width)
+    )(
+        queries,
+        suffix_kv,
+        prefix_kv,
+        hyp_prefix,
+        suffix_len,
+        prefix_len,
+        w_out,
+        hidden_in,
+        gain_attn.reshape(1, -1),
+        gain_pre.reshape(1, -1),
+    )
+    return resid.reshape(tokens, width), normed
+
+
+ARRIVALS = (
+    (((0, 1), (0, 1)), ((-1, 0), (-1, 0)), ((0, -1), (0, -1)), ((1, 0), (1, 0))),
+    (((1, 1), (1, 0)), ((-1, 1), (0, 1)), ((-1, -1), (-1, 0)), ((1, -1), (0, -1))),
+    (((2, 0), (1, 0)), ((0, 2), (0, 1)), ((2, -1), (-1, 0)), ((1, 2), (0, -1))),
+    (((2, 1), (1, 0)), ((-1, 2), (0, 1)), ((2, 2), (0, -1))),
+)
+OFFSETS = ((0, 0),) + tuple(offset for step in ARRIVALS for offset, _ in step)
+SLOT = {(dx % 4, dy % 4): i for i, (dx, dy) in enumerate(OFFSETS)}
+CHUNKS = 4
+
+
+def ffn_kernel(
+    normed,
+    w_gate,
+    w_up,
+    w_down,
+    out,
+    gate_raw,
+    up_raw,
+    down_raw,
+    down_other,
+    w_own,
+    w_send,
+    slabs,
+    block,
+    tok,
+    sib_send,
+    sib_recv,
+    hid,
+    rs_send,
+    rs_recv,
+    load_sem,
+    w_sem,
+    slab_ssem,
+    slab_rsem,
+    tok_ssem,
+    tok_rsem,
+    sib_ssem,
+    sib_rsem,
+    hid_ssem,
+    hid_rsem,
+    rs_ssem,
+    rs_rsem,
+):
+    ctx, req = lax.axis_index("ctx"), lax.axis_index("req")
+    z, y_lo = ctx // 2, lax.rem(ctx, 2)
+    x, y_hi, core = req // 4, lax.rem(req // 2, 2), lax.rem(req, 2)
+    y = y_hi * 2 + y_lo
+    nz = 8
+    half = tok.shape[2]
+    units = w_gate.shape[1]
+    blocks = 16 // CHUNKS
+    rows = tok.shape[1]
+    chunk = blocks * rows
+    plane = req * 2 + y_lo
+    mesh = pl.DeviceIdType.MESH
+
+    def chip(dx, dy):
+        there_y = lax.rem(y + dy + 4, 4)
+        return z * 2 + lax.rem(there_y, 2), lax.rem(x + dx + 4, 4) * 4 + there_y // 2 * 2
+
+    def along_z(dz):
+        return lax.rem(z + dz + nz, nz)
+
+    loads = [
+        pltpu.make_async_copy(src, dst, load_sem.at[i])
+        for i, (src, dst) in enumerate(((w_gate, gate_raw), (w_up, up_raw), (w_down, down_raw)))
+    ]
+    for load in loads:
+        load.start()
+
+    barrier = pltpu.get_barrier_semaphore()
+
+    def greet_plane(s, _):
+        there = lax.rem(plane + s, 32)
+        pl.semaphore_signal(
+            barrier, inc=1, device_id={"ctx": z * 2 + lax.rem(there, 2), "req": there // 2}, device_id_type=mesh
+        )
+        return 0
+
+    def greet_z(s, _):
+        for c in range(2):
+            pl.semaphore_signal(
+                barrier, inc=1, device_id={"ctx": along_z(s) * 2 + y_lo, "req": req - core + c}, device_id_type=mesh
+            )
+        return 0
+
+    lax.fori_loop(1, 32, greet_plane, 0)
+    lax.fori_loop(1, nz, greet_z, 0)
+    pl.semaphore_wait(barrier, 31 + 2 * (nz - 1))
+
+    def slab_copy(to_z, to_core, from_z, from_core):
+        return pltpu.make_async_remote_copy(
+            src_ref=normed.at[to_core],
+            dst_ref=slabs.at[from_core, from_z],
+            send_sem=slab_ssem.at[to_core, to_z],
+            recv_sem=slab_rsem.at[from_core, from_z],
+            device_id={"ctx": to_z * 2 + y_lo, "req": req - core + to_core},
+            device_id_type=mesh,
+        )
+
+    slab_copy(z, 1 - core, z, core).start()
+
+    def send_slab(s, _):
+        slab_copy(along_z(s), core, z, core).start()
+        slab_copy(along_z(s), 1 - core, z, core).start()
+        return 0
+
+    lax.fori_loop(1, nz, send_slab, 0)
+    slabs[core, z] = normed[core]
+
+    loads[0].wait()
+    loads[1].wait()
+    eye = (
+        lax.broadcasted_iota(jnp.int32, (units, units), 0) == lax.broadcasted_iota(jnp.int32, (units, units), 1)
+    ).astype(jnp.bfloat16)
+    piece = half // 2
+
+    def transpose_to(dst, which):
+        for i, raw in enumerate((gate_raw, up_raw)):
+            for k in range(0, half, piece):
+                part = raw[pl.ds(pl.multiple_of(which * half + k, piece), piece), :]
+                dst[i * units : (i + 1) * units, k : k + piece] = lax.dot_general(
+                    eye, part, NT, preferred_element_type=jnp.float32
+                ).astype(jnp.bfloat16)
+
+    transpose_to(w_send, 1 - core)
+    w_copy = pltpu.make_async_remote_copy(
+        src_ref=w_send,
+        dst_ref=w_own.at[pl.ds(2 * units, 2 * units), :],
+        send_sem=w_sem.at[0],
+        recv_sem=w_sem.at[1],
+        device_id={"req": req + 1 - 2 * core},
+        device_id_type=mesh,
+    )
+    w_copy.start()
+    transpose_to(w_own, core)
+    loads[2].wait()
+    down_copy = pltpu.make_async_remote_copy(
+        src_ref=down_raw.at[:, 1 - y_lo],
+        dst_ref=down_other,
+        send_sem=w_sem.at[2],
+        recv_sem=w_sem.at[3],
+        device_id={"ctx": ctx + 1 - 2 * y_lo},
+        device_id_type=mesh,
+    )
+    down_copy.start()
+
+    slab_copy(z, 1 - core, z, 1 - core).wait_recv()
+
+    def wait_slab(s, _):
+        slab_copy(along_z(s), core, along_z(s), core).wait_recv()
+        slab_copy(along_z(s), core, along_z(s), 1 - core).wait_recv()
+        return 0
+
+    lax.fori_loop(1, nz, wait_slab, 0)
+    for c in range(2):
+        for s in range(nz):
+            first = (c * nz + s) * 4
+            block[first : first + 4, :] = slabs[c, s].astype(jnp.float32)
+    tok[0] = block[...].astype(jnp.bfloat16)
+
+    def tok_copy(offset, link):
+        source = SLOT[(offset[0] - link[0]) % 4, (offset[1] - link[1]) % 4]
+        slot = SLOT[offset[0] % 4, offset[1] % 4]
+        there_ctx, there_req = chip(-link[0], -link[1])
+        return pltpu.make_async_remote_copy(
+            src_ref=tok.at[source],
+            dst_ref=tok.at[slot],
+            send_sem=tok_ssem.at[slot],
+            recv_sem=tok_rsem.at[slot],
+            device_id={"ctx": there_ctx, "req": there_req + core},
+            device_id_type=mesh,
+        )
+
+    for offset, link in ARRIVALS[0]:
+        tok_copy(offset, link).start()
+
+    def token_step(step):
+        for offset, link in ARRIVALS[step]:
+            tok_copy(offset, link).wait_recv()
+            if step + 1 < len(ARRIVALS):
+                for later, by in ARRIVALS[step + 1]:
+                    if ((later[0] - by[0] - offset[0]) % 4, (later[1] - by[1] - offset[1]) % 4) == (0, 0):
+                        tok_copy(later, by).start()
+        if step + 1 < len(ARRIVALS):
+            for later, by in ARRIVALS[step + 1]:
+                source = SLOT[(later[0] - by[0]) % 4, (later[1] - by[1]) % 4]
+                if source <= 4 * step:
+                    tok_copy(later, by).start()
+
+    def sib_copy(g):
+        return pltpu.make_async_remote_copy(
+            src_ref=sib_send.at[g],
+            dst_ref=sib_recv.at[g],
+            send_sem=sib_ssem.at[g],
+            recv_sem=sib_rsem.at[g],
+            device_id={"req": req + 1 - 2 * core},
+            device_id_type=mesh,
+        )
+
+    own_part = []
+
+    def gate_up(g):
+        tokens = tok[g * blocks : (g + 1) * blocks].reshape(chunk, half)
+        sib_send[g] = lax.dot_general(w_own[2 * units :, :], tokens, NT, preferred_element_type=jnp.float32)
+        sib_copy(g).start()
+        own_part.append(lax.dot_general(w_own[: 2 * units, :], tokens, NT, preferred_element_type=jnp.float32))
+
+    major = 1 - 2 * core
+
+    def hid_copy(g, hop, way):
+        toward = major if way == 0 else -major
+        source = along_z(-toward * (hop - 1))
+        return pltpu.make_async_remote_copy(
+            src_ref=hid.at[g, source],
+            dst_ref=hid.at[g, source],
+            send_sem=hid_ssem.at[g, hop - 1, way],
+            recv_sem=hid_rsem.at[g, source],
+            device_id={"ctx": along_z(toward) * 2 + y_lo},
+            device_id_type=mesh,
+        )
+
+    def hid_wait(g, hop, way):
+        toward = major if way == 0 else -major
+        source = along_z(-toward * hop)
+        pltpu.make_async_remote_copy(
+            src_ref=hid.at[g, source],
+            dst_ref=hid.at[g, source],
+            send_sem=hid_ssem.at[g, hop - 1, way],
+            recv_sem=hid_rsem.at[g, source],
+            device_id={"ctx": along_z(-toward) * 2 + y_lo},
+            device_id_type=mesh,
+        ).wait_recv()
+
+    hops = (nz // 2, (nz - 1) // 2)
+
+    def hidden(g):
+        sib_copy(g).wait_recv()
+        both = own_part[g] + sib_recv[g]
+        act = jax.nn.gelu(both[:units], approximate=True) * both[units:]
+        hid[g, z] = act.astype(jnp.bfloat16)
+        for way in range(2):
+            hid_copy(g, 1, way).start()
+
+    def hop(g, k):
+        for way in range(2):
+            if k - 1 <= hops[way]:
+                hid_wait(g, k - 1, way)
+                if k <= hops[way]:
+                    hid_copy(g, k, way).start()
+
+    def rs_copy(g, i, side, there_ctx, there_req, there_lo):
+        return pltpu.make_async_remote_copy(
+            src_ref=rs_send.at[g, side, pl.ds(i * 32, 32), :],
+            dst_ref=rs_recv.at[plane, pl.ds(pl.multiple_of(there_lo * 32, 32), 32), :],
+            send_sem=rs_ssem.at[g, i, side],
+            recv_sem=rs_rsem.at[plane],
+            device_id={"ctx": there_ctx, "req": there_req},
+            device_id_type=mesh,
+        )
+
+    def each_term(g, act):
+        for b in range(blocks):
+            dx, dy = OFFSETS[g * blocks + b]
+            block_ctx, first_req = chip(dx, dy)
+            lo = lax.rem(block_ctx, 2)
+            for c in range(2):
+                for side in range(2):
+                    to_ctx = ctx if side == 0 else ctx + 1 - 2 * y_lo
+                    mine = (to_ctx == ctx) & (first_req + c == req)
+                    possible = side == 0 and dx == 0 and dy in (0, 1, -1)
+                    act(g, b * 2 + c, side, to_ctx, first_req + c, lo, mine if possible else None)
+
+    def send_term(g, i, side, to_ctx, to_req, lo, mine):
+        if mine is None:
+            rs_copy(g, i, side, to_ctx, to_req, lo).start()
+            return
+
+        @pl.when(mine)
+        def _():
+            rs_recv[plane, pl.ds(pl.multiple_of(lo * 32, 32), 32), :] = rs_send[g, side, pl.ds(i * 32, 32), :]
+
+        @pl.when(jnp.logical_not(mine))
+        def _():
+            rs_copy(g, i, side, to_ctx, to_req, lo).start()
+
+    def wait_term(g, i, side, to_ctx, to_req, lo, mine):
+        if mine is None:
+            rs_copy(g, i, side, to_ctx, to_req, lo).wait_send()
+            return
+
+        @pl.when(jnp.logical_not(mine))
+        def _():
+            rs_copy(g, i, side, to_ctx, to_req, lo).wait_send()
+
+    def down(g):
+        for way in range(2):
+            if way == 0 or hops[0] == hops[1]:
+                hid_wait(g, hops[way], way)
+        act = hid[g].reshape(nz * units, chunk).T
+        for side in range(2):
+            matrix = (down_raw[:, y_lo] if side == 0 else down_other[...]).reshape(nz * units, -1)
+            rs_send[g, side] = jnp.dot(act, matrix, preferred_element_type=jnp.float32).astype(jnp.bfloat16)
+        each_term(g, send_term)
+
+    token_step(0)
+    w_copy.wait()
+    gate_up(0)
+    hidden(0)
+    hop(0, 2)
+    token_step(1)
+    gate_up(1)
+    hop(0, 3)
+    hidden(1)
+    hop(0, 4)
+    hop(1, 2)
+    token_step(2)
+    gate_up(2)
+    hop(1, 3)
+    hidden(2)
+    down_copy.wait()
+    down(0)
+    hop(1, 4)
+    hop(2, 2)
+    token_step(3)
+    gate_up(3)
+    hop(2, 3)
+    hidden(3)
+    down(1)
+    hop(2, 4)
+    hop(3, 2)
+    down(2)
+    hop(3, 3)
+    hop(3, 4)
+    down(3)
+
+    def add_terms(s, total):
+        there = lax.rem(plane + s, 32)
+        pltpu.make_async_remote_copy(
+            src_ref=rs_recv.at[there],
+            dst_ref=rs_recv.at[there],
+            send_sem=rs_ssem.at[0, 0, 0],
+            recv_sem=rs_rsem.at[there],
+            device_id={"ctx": z * 2 + lax.rem(there, 2), "req": there // 2},
+            device_id_type=mesh,
+        ).wait_recv()
+        return total + rs_recv[there].astype(jnp.float32)
+
+    total = lax.fori_loop(1, 32, add_terms, rs_recv[plane].astype(jnp.float32))
+    out[...] = total.astype(jnp.bfloat16)
+
+    slab_copy(z, 1 - core, z, core).wait_send()
+
+    def wait_sends(s, _):
+        slab_copy(along_z(s), core, z, core).wait_send()
+        slab_copy(along_z(s), 1 - core, z, core).wait_send()
+        return 0
+
+    lax.fori_loop(1, nz, wait_sends, 0)
+    for step in ARRIVALS:
+        for offset, link in step:
+            tok_copy(offset, link).wait_send()
+    for g in range(CHUNKS):
+        sib_copy(g).wait_send()
+        for way in range(2):
+            for k in range(hops[way]):
+                hid_copy(g, k + 1, way).wait_send()
+        each_term(g, wait_term)
+
+
+def ffn(normed, w_gate, w_up, w_down):
+    half = normed.shape[2]
+    units = w_gate.shape[1]
+    columns = w_down.shape[1]
+    vmem = pl.BlockSpec(memory_space=pltpu.VMEM)
+    hbm = pl.BlockSpec(memory_space=pl.ANY)
+    dma = pltpu.SemaphoreType.DMA
+    bf16 = jnp.bfloat16
+    chunk = 1024 // CHUNKS
+    return pl.pallas_call(
+        ffn_kernel,
+        out_shape=jax.ShapeDtypeStruct((64, columns), bf16),
+        in_specs=[vmem, hbm, hbm, hbm],
+        out_specs=vmem,
+        scratch_shapes=[
+            pltpu.VMEM(w_gate.shape, bf16),
+            pltpu.VMEM(w_up.shape, bf16),
+            pltpu.VMEM((8, 2, units, columns), bf16),
+            pltpu.VMEM((8, units, columns), bf16),
+            pltpu.VMEM((4 * units, half), bf16),
+            pltpu.VMEM((2 * units, half), bf16),
+            pltpu.VMEM((2, 8, 4, half), bf16),
+            pltpu.VMEM((64, half), jnp.float32),
+            pltpu.VMEM((16, 64, half), bf16),
+            pltpu.VMEM((CHUNKS, 2 * units, chunk), jnp.float32),
+            pltpu.VMEM((CHUNKS, 2 * units, chunk), jnp.float32),
+            pltpu.VMEM((CHUNKS, 8, units, chunk), bf16),
+            pltpu.VMEM((CHUNKS, 2, chunk, columns), bf16),
+            pltpu.VMEM((32, 64, columns), bf16),
+            dma((3,)),
+            dma((4,)),
+            dma((2, 8)),
+            dma((2, 8)),
+            dma((16,)),
+            dma((16,)),
+            dma((CHUNKS,)),
+            dma((CHUNKS,)),
+            dma((CHUNKS, 4, 2)),
+            dma((CHUNKS, 8)),
+            dma((CHUNKS, 8, 2)),
+            dma((32,)),
+        ],
+        compiler_params=pltpu.CompilerParams(
+            collective_id=1, has_side_effects=True, vmem_limit_bytes=56 * 2**20
+        ),
+        cost_estimate=pl.CostEstimate(flops=4 * 10**9, bytes_accessed=10**7, transcendentals=10**6),
+        name="feed_forward",
+    )(normed, w_gate, w_up, w_down.reshape(8, 2, units, columns))
 
 
 def shards(
@@ -278,25 +727,10 @@
     w_down,
 ):
     n_ctx = lax.axis_size("ctx")
-    resid = attention(
-        n_ctx, queries, suffix_kv, prefix_kv, hyp_prefix, suffix_len, prefix_len, w_out, hidden_in, gain_attn
+    resid, normed = attention(
+        n_ctx, queries, suffix_kv, prefix_kv, hyp_prefix, suffix_len, prefix_len, w_out, hidden_in, gain_attn, gain_pre
     )
-    resid_f = resid.astype(jnp.float32)
-    scale_b = lax.rsqrt(jnp.mean(resid_f * resid_f, -1, keepdims=True) + eps)
-    normed = (resid_f * scale_b * gain_pre).astype(jnp.bfloat16)
-    piece = lax.all_gather(normed, "req", axis=0, tiled=True)
-    gate = jnp.dot(piece, w_gate, preferred_element_type=jnp.float32)
-    upper = jnp.dot(piece, w_up, preferred_element_type=jnp.float32)
-    hidden = (jax.nn.gelu(gate, approximate=True) * upper).astype(jnp.bfloat16)
-    partial_out = jnp.dot(
-        lax.all_gather(hidden, "ctx", axis=1, tiled=True),
-        w_down,
-        preferred_element_type=jnp.float32,
-    )
-    ffn_out = lax.psum_scatter(partial_out, "req", scatter_dimension=0, tiled=True).astype(
-        jnp.bfloat16
-    )
-    return (resid, ffn_out)
+    return resid, ffn(normed, w_gate, w_up, w_down)
 
 
 def solution(mesh):

time: 368 us -> 174 us (0.47)
  waiting for transfers between devices: 268 us -> 0 us
  Pallas kernels: 55.3 us -> 153 us
  matrix products: 17.1 us -> 0 us
  between operations: 13.9 us -> 0.68 us
  local copies, waits for them, and re-layouts: 9.51 us -> 19.3 us
    all_gather x2 -> x0, waiting for transfers between devices: 192 us -> none  [the longest x1 106 us: shards(): lax.all_gather(hidden, 'ctx', axis=1, tiled=True)]
    pallas_call x1 -> x2, Pallas kernels: 55.3 us -> 153 us  [the longest x1 98.4 us: ffn(): pl.pallas_call(ffn_kernel, out_shape=jax.ShapeDtypeStruct((64, columns),...]
    reduce_scatter x1 -> x0, waiting for transfers between devices: 76.2 us -> none  [shards(): lax.psum_scatter(partial_out, 'req', scatter_dimension=0, tiled=True)]
    dot_general x3 -> x0, matrix products: 17.1 us -> none  [the longest x1 6.99 us: shards(): gate = jnp.dot(piece, w_gate, preferred_element_type=jnp.float32)]
    unnamed x28, local copies, waits for them, and re-layouts: 8.46 us -> 16.9 us
  transfers between devices with their start and end apart: 3 -> 0, of which waited for: 3 -> 0; matrix products, arithmetic and copies ran while one was open for 0% -> 0% of each run, Pallas kernels for 0% -> 0%
where the time goes in v2:
time: 174 us; the launch traced here: 173 us
  Pallas kernels  153 us (88%)
  local copies, waits for them, and re-layouts  19.3 us (11%)
    pallas_call x1, Pallas kernels, ffn(): pl.pallas_call(ffn_kernel, out_shape=jax.ShapeDtypeStruct((64, columns),...  98.4 us
    pallas_call x1, Pallas kernels, attention(): pl.pallas_call(functools.partial(attention_kernel, n), out_shape=(jax.Sha...  55 us
    unnamed x28, local copies, waits for them, and re-layouts  16.9 us

profile of v2, /device:TPU:1, one launch (start us, length us, event | category | flops | bytes accessed | tf_op | source)
XLA Modules:
  0.0 173.3 jit_solution(12396170100163132235)
XLA Ops:
  0.6 0.7 reshape.16.gain_attn
  1.4 0.7 reshape.17.gain_pre
  2.1 0.0 copy-start
  2.1 1.7 copy-done
  3.8 0.0 copy-start.1
  3.8 1.6 copy-done.1
  5.4 0.0 copy-start.2
  5.4 1.1 copy-done.2
  6.4 0.0 copy-start.3
  6.4 1.0 copy-done.3
  7.5 0.0 copy-start.4
  7.5 1.0 copy-done.4
  8.5 0.0 copy-start.5
  8.5 0.7 copy-done.5
  9.2 0.0 copy-start.6
  9.2 0.7 copy-done.6
  9.8 0.0 copy-start.7
  9.8 0.7 copy-done.7
  10.5 0.0 copy-start.11
  10.5 55.0 %attention_projection.1 = (bf16[16,4,4608]{2,1,0:T(4,128)(2,1)S(1)}, bf16[2,4,2304]{2,1,0:T(4,128)(2,1)S(1)}) custom-call(bf16[64,4096]{1,0:T(8,128)(2,1)S(1)} %copy-done.3, bf16[2,64,2048]{2,1,0:T(8,128)(2,1)S(1)} %copy-done.4, bf16[2,2,128,2048]{3,2,1,0:T(8,128)(2,1)S(1)} %copy-done.1, s32[4]{0:T(128)S(1)} %copy-done.5, s32[4]{0:T(128)S(1)} %copy-done.6, ...), custom_call_target="tpu_custom_call" | custom-call | flops 1000000000 | bytes 10000000 | tf_op jit(solution)/shard_map/attention_projection/pallas_call | solution.py:252
  65.5 0.0 copy-start.8
  65.5 0.6 copy-done.8
  66.1 0.0 copy-start.9
  66.1 0.9 reshape.18
  67.0 0.0 copy-done.11
  67.0 1.7 copy.15
  68.7 0.0 copy-done.9
  68.7 2.4 %copy.16.w_gate = bf16[4608,144]{1,0:T(8,128)(2,1)} copy(bf16[4608,144]{0,1:T(8,128)(2,1)S(1)} %copy-done.9) | data formatting | bytes 2654208 | tf_op args[10]
  71.1 0.0 copy-done.10
  71.1 2.4 %copy.17.w_up = bf16[4608,144]{1,0:T(8,128)(2,1)} copy(bf16[4608,144]{0,1:T(8,128)(2,1)S(1)} %copy-done.10) | data formatting | bytes 2654208 | tf_op args[11]
  73.5 98.4 %feed_forward.1 = bf16[64,288]{1,0:T(8,128)(2,1)} custom-call(bf16[2,4,2304]{2,1,0:T(4,128)(2,1)} %copy-done.8, bf16[4608,144]{1,0:T(8,128)(2,1)} %copy.16.w_gate, bf16[4608,144]{1,0:T(8,128)(2,1)} %copy.17.w_up, bf16[8,2,144,288]{3,2,1,0:T(8,128)(2,1)} %bitcast.1), custom_call_target="tpu_custom_call" | custom-call | flops 4000000000 | bytes 10000000 | tf_op jit(solution)/shard_map/feed_forward/pallas_call | solution.py:673
  171.9 1.4 copy.19
  (1 shorter events, 0.0 us)
Async XLA Ops:
  2.1 1.7 copy-start
  3.8 1.6 copy-start.1
  5.4 1.1 copy-start.2
  6.4 1.0 copy-start.3
  7.5 1.0 copy-start.4
  8.5 0.7 copy-start.5
  9.2 0.7 copy-start.6
  9.8 0.7 copy-start.7
  10.5 56.5 %copy-start.11 = (bf16[2304,288]{0,1:T(8,128)(2,1)S(1)}, bf16[2304,288]{0,1:T(8,128)(2,1)}, u32[]{:S(2)}) copy-start(bf16[2304,288]{0,1:T(8,128)(2,1)} %param.25) | copy-start | bytes 3981316
  65.5 0.6 copy-start.8
  66.1 2.6 %copy-start.9 = (bf16[4608,144]{0,1:T(8,128)(2,1)S(1)}, bf16[4608,144]{0,1:T(8,128)(2,1)}, u32[]{:S(2)}) copy-start(bf16[4608,144]{0,1:T(8,128)(2,1)} %param.23) | copy-start | bytes 3981316
  68.7 2.4 %copy-start.10 = (bf16[4608,144]{0,1:T(8,128)(2,1)S(1)}, bf16[4608,144]{0,1:T(8,128)(2,1)}, u32[]{:S(2)}) copy-start(bf16[4608,144]{0,1:T(8,128)(2,1)} %param.24) | copy-start | bytes 3981316

commit v3 on v1

v3 whole, which is shorter than its diff:
```python
import functools

import jax
import jax.numpy as jnp
from jax import lax
from jax.experimental import pallas as pl
from jax.experimental.pallas import tpu as pltpu
from jax.sharding import PartitionSpec as P

HEADS = 32
KV_HEADS = 16
HEAD = 128

softcap = 50.0
query_scale = 144.0 ** (-0.5)
eps = 1e-06

NT = (((1,), (1,)), ((), ()))
NN = (((1,), (0,)), ((), ()))


def slab_of(ctx):
    return lax.rem(ctx, 2) * 8 + ctx // 2


def weights_of(scores):
    return jnp.exp(softcap * jnp.tanh(scores * (query_scale / softcap)))


ARRIVALS = (
    (((0, 1), (0, 1)), ((-1, 0), (-1, 0)), ((0, -1), (0, -1)), ((1, 0), (1, 0))),
    (((1, 1), (1, 0)), ((-1, 1), (0, 1)), ((-1, -1), (-1, 0)), ((1, -1), (0, -1))),
    (((2, 0), (1, 0)), ((0, 2), (0, 1)), ((2, -1), (-1, 0)), ((1, 2), (0, -1))),
    (((2, 1), (1, 0)), ((-1, 2), (0, 1)), ((2, 2), (0, -1))),
)
OFFSETS = ((0, 0),) + tuple(offset for step in ARRIVALS for offset, _ in step)
SLOT = {(dx % 4, dy % 4): i for i, (dx, dy) in enumerate(OFFSETS)}
CHUNKS = 4


MESH = pl.DeviceIdType.MESH


def layer_kernel(
    queries_in,
    suffix_in,
    prefix_in,
    hyp_prefix,
    suffix_len,
    prefix_len,
    w_out_in,
    hidden_hbm,
    gain_attn_in,
    gain_pre_in,
    w_gate,
    w_up,
    w_down,
    resid_out,
    out,
    queries,
    suffix_kv,
    prefix_kv,
    w_out,
    hidden_in,
    gains,
    mask,
    part_send,
    part_recv,
    proj_send,
    proj_recv,
    normed,
    down_raw,
    down_rows,
    down_own,
    down_other,
    w_own,
    slabs,
    block,
    tok,
    sib_send,
    sib_recv,
    hid,
    rs_send,
    rs_recv,
    load_sem,
    part_ssem,
    part_rsem,
    proj_ssem,
    proj_rsem,
    resid_ssem,
    resid_rsem,
    w_ssem,
    w_rsem,
    slab_ssem,
    slab_rsem,
    tok_ssem,
    tok_rsem,
    sib_ssem,
    sib_rsem,
    hid_ssem,
    hid_rsem,
    rs_ssem,
    rs_rsem,
):
    ctx, req = lax.axis_index("ctx"), lax.axis_index("req")
    z, y_lo = ctx // 2, lax.rem(ctx, 2)
    x, y_hi, core = req // 4, lax.rem(req // 2, 2), lax.rem(req, 2)
    y = y_hi * 2 + y_lo
    plane = req * 2 + y_lo
    n = 16
    nz = 8
    tokens = queries.shape[0]
    prefixes, positions = prefix_kv.shape[1], prefix_kv.shape[2]
    group = HEADS // KV_HEADS
    rows = group * tokens
    hyps = hyp_prefix.shape[0]
    suf = tokens // hyps
    slab = tokens // n
    width = w_out.shape[1]
    half = width // 2
    units = w_gate.shape[0]
    blocks = 16 // CHUNKS
    chunk = blocks * tokens

    def chip(dx, dy):
        there_y = lax.rem(y + dy + 4, 4)
        return z * 2 + lax.rem(there_y, 2), lax.rem(x + dx + 4, 4) * 4 + there_y // 2 * 2

    def along_z(dz):
        return lax.rem(z + dz + nz, nz)

    def remote(src, dst, ssem, rsem, **where):
        return pltpu.make_async_remote_copy(
            src_ref=src, dst_ref=dst, send_sem=ssem, recv_sem=rsem, device_id=where, device_id_type=MESH
        )

    mine = pl.ds(pl.multiple_of(core * half, half), half)
    others = pl.ds(pl.multiple_of((1 - core) * half, half), half)
    gate_rows, up_rows = pl.ds(0, units), pl.ds(units, units)
    loads = [
        pltpu.make_async_copy(src, dst, load_sem.at[i])
        for i, (src, dst) in enumerate(
            (
                (queries_in, queries),
                (prefix_in, prefix_kv),
                (suffix_in, suffix_kv),
                (w_out_in, w_out),
                (hidden_hbm, hidden_in),
                (w_down, down_raw),
                (w_gate.at[:, mine], w_own.at[gate_rows, :]),
                (w_up.at[:, mine], w_own.at[up_rows, :]),
            )
        )
    ]
    for load in loads:
        load.start()

    barrier = pltpu.get_barrier_semaphore()

    def greet(there_ctx, there_req):
        pl.semaphore_signal(barrier, inc=1, device_id={"ctx": there_ctx, "req": there_req}, device_id_type=MESH)

    def greet_ctx(s, _):
        greet(lax.rem(ctx + s, n), req)
        return 0

    def greet_core(s, _):
        greet(along_z(s) * 2 + y_lo, req + 1 - 2 * core)
        return 0

    def greet_plane(s, _):
        there = lax.rem(plane + s, 32)
        there_ctx, there_req = z * 2 + lax.rem(there, 2), there // 2

        @pl.when(there_req != req)
        def _():
            greet(there_ctx, there_req)

        return 0

    lax.fori_loop(1, n, greet_ctx, 0)
    lax.fori_loop(1, nz, greet_core, 0)
    lax.fori_loop(1, 32, greet_plane, 0)

    row = lax.broadcasted_iota(jnp.int32, (rows, prefixes * positions), 0)
    col = lax.broadcasted_iota(jnp.int32, (rows, prefixes * positions), 1)
    hyp_of_row = lax.rem(row, tokens) // suf
    row_pid = jnp.zeros_like(row)
    for h in range(hyps):
        row_pid = jnp.where(hyp_of_row == h, hyp_prefix[h] - req * prefixes, row_pid)
    col_pid = col // positions
    col_len = jnp.zeros_like(row)
    for p in range(prefixes):
        col_len = jnp.where(col_pid == p, prefix_len[p], col_len)
    ok = (row_pid == col_pid) & (ctx * positions + lax.rem(col, positions) < col_len)
    mask[...] = jnp.where(ok, 1.0, 0.0)
    eye = lax.broadcasted_iota(jnp.int32, (rows, rows), 0) == lax.broadcasted_iota(jnp.int32, (rows, rows), 1)
    for i, gain in enumerate((gain_attn_in, gain_pre_in)):
        for k in range(width // 128):
            gains[i : i + 1, k * 128 : (k + 1) * 128] = gain[k : k + 1, :]

    loads[0].wait()
    loads[1].wait()
    pl.semaphore_wait(barrier, (n - 1) + (nz - 1) + 30)

    w_copies = [
        remote(
            src.at[:, others],
            w_own.at[pl.ds((2 + i) * units, units), :],
            w_ssem.at[i],
            w_rsem.at[i],
            req=req + 1 - 2 * core,
        )
        for i, src in enumerate((w_gate, w_up))
    ]
    for copy in w_copies:
        copy.start()

    def query_rows(head):
        both = queries[:, pl.ds(pl.multiple_of(head * (group * HEAD), group * HEAD), group * HEAD)]
        return jnp.concatenate([both[:, g * HEAD : (g + 1) * HEAD] for g in range(group)], 0)

    def partial_of(head):
        lanes = pl.ds(pl.multiple_of(head * HEAD, HEAD), HEAD)
        query = query_rows(head)
        keys = prefix_kv[0, :, :, lanes].reshape(prefixes * positions, HEAD)
        vals = prefix_kv[1, :, :, lanes].reshape(prefixes * positions, HEAD)
        scores = lax.dot_general(query, keys, NT, preferred_element_type=jnp.float32)
        weights = jnp.where(mask[...] > 0.5, weights_of(scores), 0.0)
        summed = jnp.dot(weights.astype(jnp.bfloat16), vals, preferred_element_type=jnp.float32)
        return summed, jnp.sum(weights, 1, keepdims=True)

    def store_partial(ref, summed, total):
        ref[0:rows, :] = summed.astype(jnp.bfloat16)
        flat = jnp.sum(jnp.where(eye, total, 0.0), 0, keepdims=True)
        high = flat.astype(jnp.bfloat16).astype(jnp.float32)
        low = flat - high
        place = lax.broadcasted_iota(jnp.int32, (16, rows), 0)
        ref[rows : rows + 16, :] = jnp.where(place == 0, high, jnp.where(place == 1, low, 0.0)).astype(
            jnp.bfloat16
        )

    def part_copy(peer, slot):
        return remote(part_send.at[peer], part_recv.at[slot], part_ssem.at[peer], part_rsem.at[slot], ctx=peer)

    at_once = 5

    def send_part(s, _):
        peers = [lax.rem(ctx + 1 + s * at_once + i, n) for i in range(at_once)]
        parts = [partial_of(peer) for peer in peers]
        for peer, part in zip(peers, parts):
            store_partial(part_send.at[peer], *part)
        for peer in peers:
            part_copy(peer, ctx).start()
        return 0

    lax.fori_loop(0, (n - 1) // at_once, send_part, 0)

    summed, total = partial_of(ctx)
    own = pl.ds(pl.multiple_of(ctx * HEAD, HEAD), HEAD)
    suf_row = lax.rem(lax.broadcasted_iota(jnp.int32, (rows, tokens), 0), tokens)
    suf_col = lax.broadcasted_iota(jnp.int32, (rows, tokens), 1)
    row_hyp, col_hyp = suf_row // suf, suf_col // suf
    length = jnp.zeros_like(suf_row)
    for h in range(hyps):
        length = jnp.where(col_hyp == h, suffix_len[h], length)
    usable = (row_hyp == col_hyp) & (suf_col <= suf_row) & (suf_col - col_hyp * suf < length)
    loads[2].wait()
    scores = lax.dot_general(query_rows(ctx), suffix_kv[0, :, own], NT, preferred_element_type=jnp.float32)
    weights = jnp.where(usable, weights_of(scores), 0.0)
    summed += jnp.dot(weights.astype(jnp.bfloat16), suffix_kv[1, :, own], preferred_element_type=jnp.float32)
    total += jnp.sum(weights, 1, keepdims=True)

    loads[5].wait()
    tile = 128
    unit = (
        lax.broadcasted_iota(jnp.int32, (tile, tile), 0) == lax.broadcasted_iota(jnp.int32, (tile, tile), 1)
    ).astype(jnp.bfloat16)
    for k in range(0, down_raw.shape[1], tile):
        down_rows[k : k + tile, :] = lax.dot_general(
            unit, down_raw[:, k : k + tile], NT, preferred_element_type=jnp.float32
        ).astype(jnp.bfloat16)
    down_copies = [
        remote(
            down_rows.at[pl.ds(pl.multiple_of((2 * s + 1 - y_lo) * units, units), units), :],
            down_other.at[pl.ds(s * units, units), :],
            w_ssem.at[2 + s],
            w_rsem.at[2 + s],
            ctx=ctx + 1 - 2 * y_lo,
        )
        for s in range(nz)
    ]
    for copy in down_copies:
        copy.start()
    for s in range(nz):
        down_own[s * units : (s + 1) * units, :] = down_rows[
            pl.ds(pl.multiple_of((2 * s + y_lo) * units, units), units), :
        ]

    def add_part(s, carry):
        summed, flat = carry
        peer = lax.rem(ctx + n - s, n)
        part_copy(peer, peer).wait_recv()
        part = part_recv.at[peer]
        return summed + part[0:rows, :].astype(jnp.float32), flat + part[rows : rows + 16, :].astype(jnp.float32)

    summed, flat = lax.fori_loop(1, n, add_part, (summed, jnp.zeros((16, rows), jnp.float32)))
    flat = jnp.sum(flat, 0, keepdims=True)
    total += jnp.sum(jnp.where(eye, flat, 0.0), 1, keepdims=True)
    attn = (summed / total).astype(jnp.bfloat16)
    attn = jnp.concatenate([attn[g * tokens : (g + 1) * tokens] for g in range(group)], 1)

    loads[3].wait()
    step = 512
    for c in range(0, width, step):
        term = jnp.dot(attn, w_out[:, c : c + step], preferred_element_type=jnp.float32)
        for i in range(n):
            proj_send[i, :, c : c + step] = term[i * slab : (i + 1) * slab].astype(jnp.bfloat16)

    def proj_copy(peer, slot):
        return remote(
            proj_send.at[slab_of(peer)], proj_recv.at[slot], proj_ssem.at[peer], proj_rsem.at[slot], ctx=peer
        )

    def send_proj(s, _):
        proj_copy(lax.rem(ctx + s, n), ctx).start()
        return 0

    lax.fori_loop(1, n, send_proj, 0)

    place = slab_of(ctx)
    loads[4].wait()
    around = hidden_in[pl.ds(pl.multiple_of(place * slab // 16 * 16, 16), 16), :].astype(jnp.float32)
    before = jnp.zeros((slab, width), jnp.float32)
    for g in range(16 // slab):
        before = jnp.where(lax.rem(place, 16 // slab) == g, around[g * slab : (g + 1) * slab], before)

    def add_proj(s, proj):
        peer = lax.rem(ctx + n - s, n)
        proj_copy(peer, peer).wait_recv()
        return proj + proj_recv[peer].astype(jnp.float32)

    proj = lax.fori_loop(1, n, add_proj, proj_send[place].astype(jnp.float32))
    scale_a = lax.rsqrt(jnp.mean(proj * proj, 1, keepdims=True) + eps)
    resid = (before + gains[0:1, :] * proj * scale_a).astype(jnp.bfloat16)
    resid_out[place] = resid
    resid = resid.astype(jnp.float32)
    scale_b = lax.rsqrt(jnp.mean(resid * resid, 1, keepdims=True) + eps)
    tokens_normed = (resid * scale_b * gains[1:2, :]).astype(jnp.bfloat16)
    for h in range(2):
        normed[h] = tokens_normed[:, h * half : (h + 1) * half]

    def slab_copy(to_z, to_core, from_z, from_core):
        return remote(
            normed.at[to_core],
            slabs.at[from_core, from_z],
            slab_ssem.at[to_core, to_z],
            slab_rsem.at[from_core, from_z],
            ctx=to_z * 2 + y_lo,
            req=req - core + to_core,
        )

    slab_copy(z, 1 - core, z, core).start()

    def send_slab(s, _):
        slab_copy(along_z(s), core, z, core).start()
        slab_copy(along_z(s), 1 - core, z, core).start()
        return 0

    lax.fori_loop(1, nz, send_slab, 0)
    slabs[core, z] = normed[core]
    slab_copy(z, 1 - core, z, 1 - core).wait_recv()

    def wait_slab(s, _):
        slab_copy(along_z(s), core, along_z(s), core).wait_recv()
        slab_copy(along_z(s), core, along_z(s), 1 - core).wait_recv()
        return 0

    lax.fori_loop(1, nz, wait_slab, 0)
    for c in range(2):
        for s in range(nz):
            first = (c * nz + s) * slab
            block[first : first + slab, :] = slabs[c, s].astype(jnp.float32)
    tok[0] = block[...].astype(jnp.bfloat16)

    def tok_copy(offset, link):
        source = SLOT[(offset[0] - link[0]) % 4, (offset[1] - link[1]) % 4]
        slot = SLOT[offset[0] % 4, offset[1] % 4]
        there_ctx, there_req = chip(-link[0], -link[1])
        return pltpu.make_async_remote_copy(
            src_ref=tok.at[source],
            dst_ref=tok.at[slot],
            send_sem=tok_ssem.at[slot],
            recv_sem=tok_rsem.at[slot],
            device_id={"ctx": there_ctx, "req": there_req + core},
            device_id_type=MESH,
        )

    for offset, link in ARRIVALS[0]:
        tok_copy(offset, link).start()

    def resid_copy(peer, which):
        which = slab_of(which)
        return remote(
            resid_out.at[which], resid_out.at[which], resid_ssem.at[peer], resid_rsem.at[which], ctx=peer
        )

    def send_resid(s, _):
        resid_copy(lax.rem(ctx + s, n), ctx).start()
        return 0

    lax.fori_loop(1, n, send_resid, 0)

    def token_step(step):
        for offset, link in ARRIVALS[step]:
            tok_copy(offset, link).wait_recv()
            if step + 1 < len(ARRIVALS):
                for later, by in ARRIVALS[step + 1]:
                    if ((later[0] - by[0] - offset[0]) % 4, (later[1] - by[1] - offset[1]) % 4) == (0, 0):
                        tok_copy(later, by).start()
        if step + 1 < len(ARRIVALS):
            for later, by in ARRIVALS[step + 1]:
                source = SLOT[(later[0] - by[0]) % 4, (later[1] - by[1]) % 4]
                if source <= 4 * step:
                    tok_copy(later, by).start()

    def sib_copy(g):
        return pltpu.make_async_remote_copy(
            src_ref=sib_send.at[g],
            dst_ref=sib_recv.at[g],
            send_sem=sib_ssem.at[g],
            recv_sem=sib_rsem.at[g],
            device_id={"req": req + 1 - 2 * core},
            device_id_type=MESH,
        )

    own_part = []

    def gate_up(g):
        tokens = tok[g * blocks : (g + 1) * blocks].reshape(chunk, half)
        sib_send[g] = lax.dot_general(w_own[2 * units :, :], tokens, NT, preferred_element_type=jnp.float32)
        sib_copy(g).start()
        own_part.append(lax.dot_general(w_own[: 2 * units, :], tokens, NT, preferred_element_type=jnp.float32))

    major = 1 - 2 * core

    def hid_copy(g, hop, way):
        toward = major if way == 0 else -major
        source = along_z(-toward * (hop - 1))
        return pltpu.make_async_remote_copy(
            src_ref=hid.at[g, source],
            dst_ref=hid.at[g, source],
            send_sem=hid_ssem.at[g, hop - 1, way],
            recv_sem=hid_rsem.at[g, source],
            device_id={"ctx": along_z(toward) * 2 + y_lo},
            device_id_type=MESH,
        )

    def hid_wait(g, hop, way):
        toward = major if way == 0 else -major
        source = along_z(-toward * hop)
        pltpu.make_async_remote_copy(
            src_ref=hid.at[g, source],
            dst_ref=hid.at[g, source],
            send_sem=hid_ssem.at[g, hop - 1, way],
            recv_sem=hid_rsem.at[g, source],
            device_id={"ctx": along_z(-toward) * 2 + y_lo},
            device_id_type=MESH,
        ).wait_recv()

    hops = (nz // 2, (nz - 1) // 2)

    def hidden(g):
        sib_copy(g).wait_recv()
        both = own_part[g] + sib_recv[g]
        act = jax.nn.gelu(both[:units], approximate=True) * both[units:]
        hid[g, z] = act.astype(jnp.bfloat16)
        for way in range(2):
            hid_copy(g, 1, way).start()

    def hop(g, k):
        for way in range(2):
            if k - 1 <= hops[way]:
                hid_wait(g, k - 1, way)
                if k <= hops[way]:
                    hid_copy(g, k, way).start()

    def rs_copy(g, i, side, there_ctx, there_req, there_lo):
        return pltpu.make_async_remote_copy(
            src_ref=rs_send.at[g, side, pl.ds(i * 32, 32), :],
            dst_ref=rs_recv.at[plane, pl.ds(pl.multiple_of(there_lo * 32, 32), 32), :],
            send_sem=rs_ssem.at[g, i, side],
            recv_sem=rs_rsem.at[plane],
            device_id={"ctx": there_ctx, "req": there_req},
            device_id_type=MESH,
        )

    def each_term(g, act):
        for b in range(blocks):
            dx, dy = OFFSETS[g * blocks + b]
            block_ctx, first_req = chip(dx, dy)
            lo = lax.rem(block_ctx, 2)
            for c in range(2):
                for side in range(2):
                    to_ctx = ctx if side == 0 else ctx + 1 - 2 * y_lo
                    mine = (to_ctx == ctx) & (first_req + c == req)
                    possible = side == 0 and dx == 0 and dy in (0, 1, -1)
                    act(g, b * 2 + c, side, to_ctx, first_req + c, lo, mine if possible else None)

    def send_term(g, i, side, to_ctx, to_req, lo, mine):
        if mine is None:
            rs_copy(g, i, side, to_ctx, to_req, lo).start()
            return

        @pl.when(mine)
        def _():
            rs_recv[plane, pl.ds(pl.multiple_of(lo * 32, 32), 32), :] = rs_send[g, side, pl.ds(i * 32, 32), :]

        @pl.when(jnp.logical_not(mine))
        def _():
            rs_copy(g, i, side, to_ctx, to_req, lo).start()

    def wait_term(g, i, side, to_ctx, to_req, lo, mine):
        if mine is None:
            rs_copy(g, i, side, to_ctx, to_req, lo).wait_send()
            return

        @pl.when(jnp.logical_not(mine))
        def _():
            rs_copy(g, i, side, to_ctx, to_req, lo).wait_send()

    def down(g):
        for way in range(2):
            if way == 0 or hops[0] == hops[1]:
                hid_wait(g, hops[way], way)
        act = hid[g].reshape(nz * units, chunk).T
        for side in range(2):
            matrix = down_own[...] if side == 0 else down_other[...]
            rs_send[g, side] = jnp.dot(act, matrix, preferred_element_type=jnp.float32).astype(jnp.bfloat16)
        each_term(g, send_term)

    token_step(0)
    for copy in w_copies:
        copy.wait()
    loads[6].wait()
    loads[7].wait()
    gate_up(0)
    hidden(0)
    hop(0, 2)
    token_step(1)
    gate_up(1)
    hop(0, 3)
    hidden(1)
    hop(0, 4)
    hop(1, 2)
    token_step(2)
    gate_up(2)
    hop(1, 3)
    hidden(2)
    for copy in down_copies:
        copy.wait()
    down(0)
    hop(1, 4)
    hop(2, 2)
    token_step(3)
    gate_up(3)
    hop(2, 3)
    hidden(3)
    down(1)
    hop(2, 4)
    hop(3, 2)
    down(2)
    hop(3, 3)
    hop(3, 4)
    down(3)

    def add_terms(s, total):
        there = lax.rem(plane + s, 32)
        pltpu.make_async_remote_copy(
            src_ref=rs_recv.at[there],
            dst_ref=rs_recv.at[there],
            send_sem=rs_ssem.at[0, 0, 0],
            recv_sem=rs_rsem.at[there],
            device_id={"ctx": z * 2 + lax.rem(there, 2), "req": there // 2},
            device_id_type=MESH,
        ).wait_recv()
        return total + rs_recv[there].astype(jnp.float32)

    total = lax.fori_loop(1, 32, add_terms, rs_recv[plane].astype(jnp.float32))
    out[...] = total.astype(jnp.bfloat16)

    slab_copy(z, 1 - core, z, core).wait_send()

    def wait_sends(s, _):
        slab_copy(along_z(s), core, z, core).wait_send()
        slab_copy(along_z(s), 1 - core, z, core).wait_send()
        return 0

    lax.fori_loop(1, nz, wait_sends, 0)

    def finish(s, _):
        peer = lax.rem(ctx + s, n)
        resid_copy(peer, peer).wait_recv()
        part_copy(peer, ctx).wait_send()
        proj_copy(peer, ctx).wait_send()
        resid_copy(peer, ctx).wait_send()
        return 0

    lax.fori_loop(1, n, finish, 0)
    for step in ARRIVALS:
        for offset, link in step:
            tok_copy(offset, link).wait_send()
    for g in range(CHUNKS):
        sib_copy(g).wait_send()
        for way in range(2):
            for k in range(hops[way]):
                hid_copy(g, k + 1, way).wait_send()
        each_term(g, wait_term)


def layer(
    hidden_in,
    queries,
    suffix_kv,
    prefix_kv,
    hyp_prefix,
    suffix_len,
    prefix_len,
    w_out,
    gain_attn,
    gain_pre,
    w_gate,
    w_up,
    w_down,
):
    n = 16
    tokens, width = hidden_in.shape
    half = width // 2
    rows = HEADS // KV_HEADS * tokens
    slab = tokens // n
    positions = prefix_kv.shape[1] * prefix_kv.shape[2]
    units = w_gate.shape[1]
    columns = w_down.shape[1]
    chunk = 16 // CHUNKS * tokens
    vmem = pl.BlockSpec(memory_space=pltpu.VMEM)
    smem = pl.BlockSpec(memory_space=pltpu.SMEM)
    hbm = pl.BlockSpec(memory_space=pl.ANY)
    dma = pltpu.SemaphoreType.DMA
    bf16 = jnp.bfloat16
    resid, out = pl.pallas_call(
        layer_kernel,
        out_shape=(
            jax.ShapeDtypeStruct((n, slab, width), bf16),
            jax.ShapeDtypeStruct((tokens, columns), bf16),
        ),
        in_specs=[hbm, hbm, hbm, smem, smem, smem, hbm, hbm, vmem, vmem, hbm, hbm, hbm],
        out_specs=(vmem, vmem),
        scratch_shapes=[
            pltpu.VMEM(queries.shape, bf16),
            pltpu.VMEM(suffix_kv.shape, bf16),
            pltpu.VMEM(prefix_kv.shape, bf16),
            pltpu.VMEM(w_out.shape, bf16),
            pltpu.VMEM(hidden_in.shape, bf16),
            pltpu.VMEM((2, width), jnp.float32),
            pltpu.VMEM((rows, positions), jnp.float32),
            pltpu.VMEM((n, rows + 16, HEAD), bf16),
            pltpu.VMEM((n, rows + 16, HEAD), bf16),
            pltpu.VMEM((n, slab, width), bf16),
            pltpu.VMEM((n, slab, width), bf16),
            pltpu.VMEM((2, slab, half), bf16),
            pltpu.VMEM((columns, n * units), bf16),
            pltpu.VMEM((n * units, columns), bf16),
            pltpu.VMEM((8 * units, columns), bf16),
            pltpu.VMEM((8 * units, columns), bf16),
            pltpu.VMEM((4 * units, half), bf16),
            pltpu.VMEM((2, 8, slab, half), bf16),
            pltpu.VMEM((tokens, half), jnp.float32),
            pltpu.VMEM((16, tokens, half), bf16),
            pltpu.VMEM((CHUNKS, 2 * units, chunk), jnp.float32),
            pltpu.VMEM((CHUNKS, 2 * units, chunk), jnp.float32),
            pltpu.VMEM((CHUNKS, 8, units, chunk), bf16),
            pltpu.VMEM((CHUNKS, 2, chunk, columns), bf16),
            pltpu.VMEM((32, tokens, columns), bf16),
            dma((8,)),
            dma((n,)),
            dma((n,)),
            dma((n,)),
            dma((n,)),
            dma((n,)),
            dma((n,)),
            dma((10,)),
            dma((10,)),
            dma((2, 8)),
            dma((2, 8)),
            dma((16,)),
            dma((16,)),
            dma((CHUNKS,)),
            dma((CHUNKS,)),
            dma((CHUNKS, 4, 2)),
            dma((CHUNKS, 8)),
            dma((CHUNKS, 8, 2)),
            dma((32,)),
        ],
        compiler_params=pltpu.CompilerParams(
            collective_id=0, has_side_effects=True, vmem_limit_bytes=60 * 2**20
        ),
        cost_estimate=pl.CostEstimate(flops=5 * 10**9, bytes_accessed=10**7, transcendentals=10**6),
        name="layer",
    )(
        queries,
        suffix_kv,
        prefix_kv,
        hyp_prefix,
        suffix_len,
        prefix_len,
        w_out,
        hidden_in,
        gain_attn.reshape(-1, 128),
        gain_pre.reshape(-1, 128),
        w_gate.T,
        w_up.T,
        w_down.T,
    )
    return resid.reshape(tokens, width), out


def solution(mesh):
    placed = (
        P("req", None),
        P("req", None),
        P(None, "req", None),
        P(None, "req", "ctx", None),
        P("req"),
        P("req"),
        P("req"),
        P("ctx", None),
        P(),
        P(),
        P(None, ("req", "ctx")),
        P(None, ("req", "ctx")),
        P("req", "ctx"),
    )
    return jax.shard_map(
        layer,
        mesh=mesh,
        in_specs=placed,
        out_specs=(P("req", None), P("req", "ctx")),
        check_vma=False,
    )
```

time: 368 us -> 132 us (0.36)
  waiting for transfers between devices: 268 us -> 0 us
  Pallas kernels: 55.3 us -> 128 us
  matrix products: 17.1 us -> 0 us
  between operations: 13.9 us -> 0.64 us
  local copies, waits for them, and re-layouts: 9.51 us -> 3.44 us
    all_gather x2 -> x0, waiting for transfers between devices: 192 us -> none  [the longest x1 106 us: shards(): lax.all_gather(hidden, 'ctx', axis=1, tiled=True)]
    reduce_scatter x1 -> x0, waiting for transfers between devices: 76.2 us -> none  [shards(): lax.psum_scatter(partial_out, 'req', scatter_dimension=0, tiled=True)]
    pallas_call x1, Pallas kernels: 55.3 us -> 128 us  [layer(): pl.pallas_call(layer_kernel, out_shape=(jax.ShapeDtypeStruct((n, slab, wi...]
    dot_general x3 -> x0, matrix products: 17.1 us -> none  [the longest x1 6.99 us: shards(): gate = jnp.dot(piece, w_gate, preferred_element_type=jnp.float32)]
    unnamed x28 -> x1, local copies, waits for them, and re-layouts: 8.46 us -> 1.42 us
  transfers between devices with their start and end apart: 3 -> 0, of which waited for: 3 -> 0; matrix products, arithmetic and copies ran while one was open for 0% -> 0% of each run, Pallas kernels for 0% -> 0%
where the time goes in v3:
time: 132 us
  Pallas kernels  128 us (97%)
  local copies, waits for them, and re-layouts  3.44 us (3%)
    pallas_call x1, Pallas kernels, layer(): pl.pallas_call(layer_kernel, out_shape=(jax.ShapeDtypeStruct((n, slab, wi...  128 us

profile of v3, /device:TPU:1, one launch (start us, length us, event | category | flops | bytes accessed | tf_op | source)
XLA Modules:
  0.0 131.9 jit_solution(16227090088488099548)
XLA Ops:
  0.6 127.8 %layer.1 = (bf16[16,4,4608]{2,1,0:T(4,128)(2,1)}, bf16[64,288]{1,0:T(8,128)(2,1)}) custom-call(bf16[64,4096]{1,0:T(8,128)(2,1)} %queries_in.1, bf16[2,64,2048]{2,1,0:T(8,128)(2,1)} %suffix_in.1, bf16[2,2,128,2048]{3,2,1,0:T(8,128)(2,1)} %prefix_in.1, s32[4]{0:T(128)} %hyp_prefix.1, s32[4]{0:T(128)} %suffix_len.1, s32[2]{0:T(128)} %prefix_len.1, ...), custom_call_target="tpu_custom_call" | custom-call | flops 5000000000 | bytes 10000000 | tf_op jit(solution)/shard_map/layer/pallas_call | solution.py:650
  128.4 2.0 %reshape.15 = bf16[64,4608]{1,0:T(8,128)(2,1)} reshape(bf16[16,4,4608]{2,1,0:T(4,128)(2,1)} %get-tuple-element.4) | data formatting | bytes 1179648 | tf_op jit(solution)/shard_map/reshape | solution.py:724
  130.4 1.4 %copy.16 = bf16[64,288]{1,0:T(8,128)(2,1)} copy(bf16[64,288]{1,0:T(8,128)(2,1)} %get-tuple-element.9) | data formatting | bytes 73728

commit v4 on v3

v4 whole, which is shorter than its diff:
```python
import functools

import jax
import jax.numpy as jnp
from jax import lax
from jax.experimental import pallas as pl
from jax.experimental.pallas import tpu as pltpu
from jax.sharding import PartitionSpec as P

HEADS = 32
KV_HEADS = 16
HEAD = 128

softcap = 50.0
query_scale = 144.0 ** (-0.5)
eps = 1e-06

NT = (((1,), (1,)), ((), ()))
MESH = pl.DeviceIdType.MESH

ARRIVALS = (
    (((0, 1), (0, 1)), ((-1, 0), (-1, 0)), ((0, -1), (0, -1)), ((1, 0), (1, 0))),
    (((1, 1), (1, 0)), ((-1, 1), (0, 1)), ((-1, -1), (-1, 0)), ((1, -1), (0, -1))),
    (((2, 0), (1, 0)), ((0, 2), (0, 1)), ((2, -1), (-1, 0)), ((1, 2), (0, -1))),
    (((2, 1), (1, 0)), ((-1, 2), (0, 1)), ((2, 2), (0, -1))),
)
OFFSETS = ((0, 0),) + tuple(offset for step in ARRIVALS for offset, _ in step)
SLOT = {(dx % 4, dy % 4): i for i, (dx, dy) in enumerate(OFFSETS)}
CHUNKS = 4
FAR_FIRST = (4, 3, 5, 2, 6, 1, 7, 0)


def weights_of(scores):
    return jnp.exp(softcap * jnp.tanh(scores * (query_scale / softcap)))


def layer_kernel(
    queries_in,
    suffix_in,
    prefix_in,
    hyp_prefix,
    suffix_len,
    prefix_len,
    w_out_in,
    hidden_hbm,
    gain_attn_in,
    gain_pre_in,
    w_gate,
    w_up,
    w_down,
    resid_out,
    out,
    queries,
    suffix_kv,
    prefix_kv,
    w_out,
    hidden_in,
    gains,
    mask,
    party_send,
    party_recv,
    part_own,
    partz_send,
    partz_recv,
    proj_send,
    projy_recv,
    projz_send,
    projz_recv,
    slab_own,
    down_raw,
    down_rows,
    down_own,
    down_other,
    w_own,
    slabs,
    block,
    tok,
    sib_send,
    sib_recv,
    hid,
    ds_send,
    ds_recv,
    rs_send,
    rs_recv,
    load_sem,
    party_sem,
    partz_sem,
    projy_sem,
    projz_sem,
    resid_sem,
    w_sem,
    slab_ssem,
    slab_rsem,
    tok_sem,
    sib_sem,
    hid_ssem,
    hid_rsem,
    ds_sem,
    rs_ssem,
    rs_rsem,
):
    ctx, req = lax.axis_index("ctx"), lax.axis_index("req")
    z, y_lo = ctx // 2, lax.rem(ctx, 2)
    x, y_hi, core = req // 4, lax.rem(req // 2, 2), lax.rem(req, 2)
    y = y_hi * 2 + y_lo
    place = x * 4 + y
    n = 16
    nz = 8
    tokens = queries.shape[0]
    prefixes, positions = prefix_kv.shape[1], prefix_kv.shape[2]
    group = HEADS // KV_HEADS
    rows = group * tokens
    hyps = hyp_prefix.shape[0]
    suf = tokens // hyps
    slab = tokens // n
    width = w_out.shape[1]
    half = width // 2
    units = w_gate.shape[0]
    blocks = 16 // CHUNKS
    part = tokens // 2
    chunk = blocks * part
    partner = ctx + 1 - 2 * y_lo
    sibling = req + 1 - 2 * core

    def chip(dx, dy):
        there_y = lax.rem(y + dy + 4, 4)
        return z * 2 + lax.rem(there_y, 2), lax.rem(x + dx + 4, 4) * 4 + there_y // 2 * 2

    def along_z(dz):
        return lax.rem(z + dz + nz, nz)

    def remote(src, dst, ssem, rsem, **where):
        return pltpu.make_async_remote_copy(
            src_ref=src, dst_ref=dst, send_sem=ssem, recv_sem=rsem, device_id=where, device_id_type=MESH
        )

    mine = pl.ds(pl.multiple_of(core * half, half), half)
    others = pl.ds(pl.multiple_of((1 - core) * half, half), half)
    loads = [
        pltpu.make_async_copy(src, dst, load_sem.at[i])
        for i, (src, dst) in enumerate(
            (
                (queries_in, queries),
                (prefix_in, prefix_kv),
                (suffix_in, suffix_kv),
                (w_out_in, w_out),
                (hidden_hbm, hidden_in),
                (w_down, down_raw),
                (w_gate.at[:, mine], w_own.at[pl.ds(0, units), :]),
                (w_up.at[:, mine], w_own.at[pl.ds(units, units), :]),
            )
        )
    ]
    for load in loads:
        load.start()

    barrier = pltpu.get_barrier_semaphore()

    def greet(there_ctx, there_req):
        pl.semaphore_signal(barrier, inc=1, device_id={"ctx": there_ctx, "req": there_req}, device_id_type=MESH)

    def greet_ctx(s, _):
        greet(lax.rem(ctx + s, n), req)
        return 0

    def greet_core(s, _):
        greet(along_z(s) * 2 + y_lo, sibling)
        return 0

    def greet_plane(s, _):
        there = lax.rem(place + s, 16)
        there_ctx, there_req = z * 2 + lax.rem(there, 2), there // 2 * 2 + core

        @pl.when(there_req != req)
        def _():
            greet(there_ctx, there_req)

        return 0

    lax.fori_loop(1, n, greet_ctx, 0)
    lax.fori_loop(0, nz, greet_core, 0)
    lax.fori_loop(1, 16, greet_plane, 0)

    row = lax.broadcasted_iota(jnp.int32, (rows, prefixes * positions), 0)
    col = lax.broadcasted_iota(jnp.int32, (rows, prefixes * positions), 1)
    hyp_of_row = lax.rem(row, tokens) // suf
    row_pid = jnp.zeros_like(row)
    for h in range(hyps):
        row_pid = jnp.where(hyp_of_row == h, hyp_prefix[h] - req * prefixes, row_pid)
    col_pid = col // positions
    col_len = jnp.zeros_like(row)
    for p in range(prefixes):
        col_len = jnp.where(col_pid == p, prefix_len[p], col_len)
    ok = (row_pid == col_pid) & (ctx * positions + lax.rem(col, positions) < col_len)
    mask[...] = jnp.where(ok, 1.0, 0.0)
    eye = lax.broadcasted_iota(jnp.int32, (rows, rows), 0) == lax.broadcasted_iota(jnp.int32, (rows, rows), 1)
    for k in range(width // 128):
        gains[0:1, k * 128 : (k + 1) * 128] = gain_attn_in[k : k + 1, :]
    for k in range(half // 128):
        gains[1:2, k * 128 : (k + 1) * 128] = jnp.where(
            core == 0, gain_pre_in[k : k + 1, :], gain_pre_in[half // 128 + k : half // 128 + k + 1, :]
        )

    def query_rows(head):
        both = queries[:, pl.ds(pl.multiple_of(head * (group * HEAD), group * HEAD), group * HEAD)]
        return jnp.concatenate([both[:, g * HEAD : (g + 1) * HEAD] for g in range(group)], 0)

    def partial_of(head):
        lanes = pl.ds(pl.multiple_of(head * HEAD, HEAD), HEAD)
        query = query_rows(head)
        keys = prefix_kv[0, :, :, lanes].reshape(prefixes * positions, HEAD)
        vals = prefix_kv[1, :, :, lanes].reshape(prefixes * positions, HEAD)
        scores = lax.dot_general(query, keys, NT, preferred_element_type=jnp.float32)
        weights = jnp.where(mask[...] > 0.5, weights_of(scores), 0.0)
        summed = jnp.dot(weights.astype(jnp.bfloat16), vals, preferred_element_type=jnp.float32)
        total = jnp.sum(weights, 1, keepdims=True)
        return summed, jnp.sum(jnp.where(eye, total, 0.0), 0, keepdims=True)

    def store_partial(ref, summed, flat):
        high = flat.astype(jnp.bfloat16).astype(jnp.float32)
        low = flat - high
        line = lax.broadcasted_iota(jnp.int32, (16, rows), 0)
        ref[0:rows, :] = summed.astype(jnp.bfloat16)
        ref[rows : rows + 16, :] = jnp.where(line == 0, high, jnp.where(line == 1, low, 0.0)).astype(jnp.bfloat16)

    def load_partial(ref):
        return (
            ref[0:rows, :].astype(jnp.float32),
            jnp.sum(ref[rows : rows + 16, :].astype(jnp.float32), 0, keepdims=True),
        )

    def distance(i):
        step = (i + 1) // 2
        return nz // 2 + step * (1 - 2 * lax.rem(i, 2))

    at_once = 4

    def others_heads(s, _):
        which = [distance(s * at_once + i) for i in range(at_once)]
        terms = [partial_of(along_z(dz) * 2 + 1 - y_lo) for dz in which]
        for dz, term in zip(which, terms):
            store_partial(party_send.at[dz], *term)
        return 0

    def own_heads(s, _):
        which = [distance(s * at_once + i) for i in range(at_once)]
        terms = [partial_of(along_z(dz) * 2 + y_lo) for dz in which]
        for dz, (summed, flat) in zip(which, terms):
            part_own[dz, 0:rows, :] = summed
            part_own[dz, rows : rows + 8, :] = jnp.broadcast_to(flat, (8, rows))
        return 0

    def party_copy(dz):
        return remote(party_send.at[dz], party_recv.at[dz], party_sem.at[0, dz], party_sem.at[1, dz], ctx=partner)

    def partz_copy(dz):
        return remote(
            partz_send.at[dz],
            partz_recv.at[dz],
            partz_sem.at[0, dz],
            partz_sem.at[1, dz],
            ctx=along_z(dz) * 2 + y_lo,
        )

    loads[0].wait()
    loads[1].wait()
    lax.fori_loop(0, nz // at_once, others_heads, 0)
    pl.semaphore_wait(barrier, (n - 1) + nz + 14)
    for dz in FAR_FIRST:
        party_copy(dz).start()

    w_copies = [
        remote(
            src.at[:, others],
            w_own.at[pl.ds((2 + i) * units, units), :],
            w_sem.at[0, i],
            w_sem.at[1, i],
            req=sibling,
        )
        for i, src in enumerate((w_gate, w_up))
    ]
    for copy in w_copies:
        copy.start()
    lax.fori_loop(0, nz // at_once, own_heads, 0)

    own = pl.ds(pl.multiple_of(ctx * HEAD, HEAD), HEAD)
    suf_row = lax.rem(lax.broadcasted_iota(jnp.int32, (rows, tokens), 0), tokens)
    suf_col = lax.broadcasted_iota(jnp.int32, (rows, tokens), 1)
    row_hyp, col_hyp = suf_row // suf, suf_col // suf
    length = jnp.zeros_like(suf_row)
    for h in range(hyps):
        length = jnp.where(col_hyp == h, suffix_len[h], length)
    usable = (row_hyp == col_hyp) & (suf_col <= suf_row) & (suf_col - col_hyp * suf < length)
    loads[2].wait()
    scores = lax.dot_general(query_rows(ctx), suffix_kv[0, :, own], NT, preferred_element_type=jnp.float32)
    weights = jnp.where(usable, weights_of(scores), 0.0)
    suf_sum = jnp.dot(weights.astype(jnp.bfloat16), suffix_kv[1, :, own], preferred_element_type=jnp.float32)
    suf_total = jnp.sum(weights, 1, keepdims=True)

    for dz in FAR_FIRST[:-1]:
        party_copy(dz).wait_recv()
        summed, flat = load_partial(party_recv.at[dz])
        store_partial(
            partz_send.at[dz], summed + part_own[dz, 0:rows, :], flat + part_own[dz, rows : rows + 1, :]
        )
        partz_copy(dz).start()

    loads[5].wait()
    tile = 128
    unit = (
        lax.broadcasted_iota(jnp.int32, (tile, tile), 0) == lax.broadcasted_iota(jnp.int32, (tile, tile), 1)
    ).astype(jnp.bfloat16)
    for k in range(0, down_raw.shape[1], tile):
        down_rows[k : k + tile, :] = lax.dot_general(
            unit, down_raw[:, k : k + tile], NT, preferred_element_type=jnp.float32
        ).astype(jnp.bfloat16)
    down_copies = [
        remote(
            down_rows.at[pl.ds(pl.multiple_of((2 * s + 1 - y_lo) * units, units), units), :],
            down_other.at[pl.ds(s * units, units), :],
            w_sem.at[0, 2 + s],
            w_sem.at[1, 2 + s],
            ctx=partner,
        )
        for s in range(nz)
    ]
    for copy in down_copies[: nz // 2]:
        copy.start()
    for s in range(nz):
        down_own[s * units : (s + 1) * units, :] = down_rows[
            pl.ds(pl.multiple_of((2 * s + y_lo) * units, units), units), :
        ]

    party_copy(0).wait_recv()
    summed, flat = load_partial(party_recv.at[0])
    summed += part_own[0, 0:rows, :] + suf_sum
    flat += part_own[0, rows : rows + 1, :]
    for dz in FAR_FIRST[:-1]:
        partz_copy(dz).wait_recv()
        more, more_flat = load_partial(partz_recv.at[dz])
        summed += more
        flat += more_flat
    total = suf_total + jnp.sum(jnp.where(eye, flat, 0.0), 1, keepdims=True)
    attn = (summed / total).astype(jnp.bfloat16)
    attn = jnp.concatenate([attn[g * tokens : (g + 1) * tokens] for g in range(group)], 1)

    loads[3].wait()
    step = 512
    for c in range(0, width, step):
        term = jnp.dot(attn, w_out[:, c : c + step], preferred_element_type=jnp.float32)
        for i in range(n):
            proj_send[i, :, c : c + step] = term[i * slab : (i + 1) * slab].astype(jnp.bfloat16)

    def projy_copy(dz):
        return remote(
            proj_send.at[(1 - y_lo) * nz + along_z(dz)],
            projy_recv.at[dz],
            projy_sem.at[0, dz],
            projy_sem.at[1, dz],
            ctx=partner,
        )

    def projz_copy(dz):
        return remote(
            projz_send.at[dz],
            projz_recv.at[dz],
            projz_sem.at[0, dz],
            projz_sem.at[1, dz],
            ctx=along_z(dz) * 2 + y_lo,
        )

    for dz in FAR_FIRST:
        projy_copy(dz).start()

    first = y_lo * nz + z
    loads[4].wait()
    around = hidden_in[pl.ds(pl.multiple_of(first * slab // 16 * 16, 16), 16), :].astype(jnp.float32)
    before = jnp.zeros((slab, width), jnp.float32)
    for g in range(16 // slab):
        before = jnp.where(lax.rem(first, 16 // slab) == g, around[g * slab : (g + 1) * slab], before)

    for dz in FAR_FIRST[:-1]:
        projy_copy(dz).wait_recv()
        both = projy_recv[dz].astype(jnp.float32) + proj_send[y_lo * nz + along_z(dz)].astype(jnp.float32)
        projz_send[dz] = both.astype(jnp.bfloat16)
        projz_copy(dz).start()

    for copy in w_copies:
        copy.wait()
    loads[6].wait()
    loads[7].wait()

    def gain_rows(i, _):
        at = pl.ds(pl.multiple_of(i * 16, 16), 16)
        w_own[at, :] = (w_own[at, :].astype(jnp.float32) * gains[1:2, :half]).astype(jnp.bfloat16)
        return 0

    lax.fori_loop(0, 4 * units // 16, gain_rows, 0)

    projy_copy(0).wait_recv()
    proj = projy_recv[0].astype(jnp.float32) + proj_send[first].astype(jnp.float32)
    for dz in FAR_FIRST[:-1]:
        projz_copy(dz).wait_recv()
        proj += projz_recv[dz].astype(jnp.float32)
    scale_a = lax.rsqrt(jnp.mean(proj * proj, 1, keepdims=True) + eps)
    resid = (before + gains[0:1, :] * proj * scale_a).astype(jnp.bfloat16)
    for h in range(2):
        slab_own[h] = resid[:, h * half : (h + 1) * half]

    def slab_copy(to_z, to_core, from_z, from_core):
        return remote(
            slab_own.at[to_core],
            slabs.at[from_core, from_z],
            slab_ssem.at[to_core, to_z],
            slab_rsem.at[from_core, from_z],
            ctx=to_z * 2 + y_lo,
            req=req - core + to_core,
        )

    for dz in FAR_FIRST[:-1]:
        slab_copy(along_z(dz), core, z, core).start()
        slab_copy(along_z(dz), 1 - core, z, core).start()
    slab_copy(z, 1 - core, z, core).start()
    for copy in down_copies[nz // 2 :]:
        copy.start()
    slabs[core, z] = slab_own[core]
    slab_copy(z, 1 - core, z, 1 - core).wait_recv()
    for dz in FAR_FIRST[:-1]:
        slab_copy(along_z(dz), core, along_z(dz), core).wait_recv()
        slab_copy(along_z(dz), core, along_z(dz), 1 - core).wait_recv()
    for c in range(2):
        for s in range(nz):
            at = (c * nz + s) * slab
            block[at : at + slab, :] = slabs[c, s].astype(jnp.float32)
        tok[c, 0] = block[c * part : (c + 1) * part, :].astype(jnp.bfloat16)

    def tok_copy(offset, link, sub):
        source = SLOT[(offset[0] - link[0]) % 4, (offset[1] - link[1]) % 4]
        slot = SLOT[offset[0] % 4, offset[1] % 4]
        there_ctx, there_req = chip(-link[0], -link[1])
        return remote(
            tok.at[sub, source],
            tok.at[sub, slot],
            tok_sem.at[0, sub, slot],
            tok_sem.at[1, sub, slot],
            ctx=there_ctx,
            req=there_req + core,
        )

    def token_step(step, sub):
        later_copies = []
        if step + 1 < len(ARRIVALS):
            for offset, link in ARRIVALS[step + 1]:
                source = SLOT[(offset[0] - link[0]) % 4, (offset[1] - link[1]) % 4]
                later_copies.append((source, tok_copy(offset, link, sub)))
        for offset, link in ARRIVALS[step]:
            tok_copy(offset, link, sub).wait_recv()
            for source, copy in later_copies:
                if source == SLOT[offset[0] % 4, offset[1] % 4]:
                    copy.start()
        for source, copy in later_copies:
            if source <= 4 * step:
                copy.start()

    def sib_copy(g, lanes):
        which = CHUNKS - 1 + lanes.start // chunk if lanes.size == chunk else g
        return remote(
            sib_send.at[g, :, lanes],
            sib_recv.at[g, :, lanes],
            sib_sem.at[0, which],
            sib_sem.at[1, which],
            req=sibling,
        )

    whole = (pl.ds(0, 2 * chunk),)
    halves = (pl.ds(0, chunk), pl.ds(chunk, chunk))
    own_part = {}
    ones = jnp.ones((16, half), jnp.bfloat16)

    def gate_up(g, lanes):
        if lanes.size == chunk:
            those = tok[lanes.start // chunk, g * blocks : (g + 1) * blocks].reshape(chunk, half)
        else:
            those = tok[:, g * blocks : (g + 1) * blocks].reshape(2 * chunk, half)
        squares = lax.dot_general(ones, those * those, NT, preferred_element_type=jnp.float32)[:8]
        sib_send[g, 2 * units :, lanes] = squares
        sib_send[g, : 2 * units, lanes] = lax.dot_general(
            w_own[2 * units :, :], those, NT, preferred_element_type=jnp.float32
        )
        sib_copy(g, lanes).start()
        products = lax.dot_general(w_own[: 2 * units, :], those, NT, preferred_element_type=jnp.float32)
        own_part[g, lanes.start] = products, squares

    major = 1 - 2 * core

    def hid_copy(g, lanes, origin, by, to):
        c = slice(None) if lanes.size != chunk else lanes.start // chunk
        which = CHUNKS - 1 + lanes.start // chunk if lanes.size == chunk else g
        source = along_z(origin)
        ref = hid.at[g, source] if lanes.size != chunk else hid.at[g, source, c]
        return remote(
            ref,
            ref,
            hid_ssem.at[which, lax.rem(to - origin + 2 * nz, nz)],
            hid_rsem.at[which, source],
            ctx=along_z(to) * 2 + y_lo,
        )

    def hidden(g, lanes):
        sib_copy(g, lanes).wait_recv()
        products, squares = own_part[g, lanes.start]
        both = products + sib_recv[g, : 2 * units, lanes]
        scale = lax.rsqrt((squares + sib_recv[g, 2 * units :, lanes])[0:1] * (1.0 / width) + eps)
        act = jax.nn.gelu(both[:units] * scale, approximate=True) * (both[units:] * scale)
        act = act.astype(jnp.bfloat16)
        for i in range(lanes.size // chunk):
            hid[g, z, lanes.start // chunk + i] = act[:, i * chunk : (i + 1) * chunk]
        for to in (2, -2, 1, -1):
            hid_copy(g, lanes, 0, 0, to).start()

    def pass_on(g, lanes):
        for way in (1, -1):
            hid_copy(g, lanes, -2 * way, 0, 0).wait_recv()

            @pl.when(major == way)
            def _():
                hid_copy(g, lanes, -2 * way, 0, 2 * way).start()

            hid_copy(g, lanes, -2 * way, 0, way).start()

    def hid_arrive(g, lanes):
        for origin in (-1, 1, -3, 3, 4):
            hid_copy(g, lanes, origin, 0, 0).wait_recv()

    def hid_sent(g, lanes):
        for to in (2, -2, 1, -1):
            hid_copy(g, lanes, 0, 0, to).wait_send()
        for way in (1, -1):

            @pl.when(major == way)
            def _():
                hid_copy(g, lanes, -2 * way, 0, 2 * way).wait_send()

            hid_copy(g, lanes, -2 * way, 0, way).wait_send()

    def ds_copy(g):
        return remote(ds_send.at[g], ds_recv.at[g], ds_sem.at[0, g], ds_sem.at[1, g], req=sibling)

    def down_terms(g, c):
        act = hid[g, :, c].reshape(nz * units, chunk).T
        return [
            jnp.dot(act, matrix[...], preferred_element_type=jnp.float32) for matrix in (down_own, down_other)
        ]

    def down(g, all_lanes):
        for lanes in all_lanes:
            hid_arrive(g, lanes)
        for side, term in enumerate(down_terms(g, 1 - core)):
            ds_send[g, side] = term.astype(jnp.bfloat16)
        ds_copy(g).start()
        return down_terms(g, core)

    def rs_copy(g, b, side):
        dx, dy = OFFSETS[g * blocks + b]
        block_ctx, first_req = chip(dx, dy)
        lo = lax.rem(block_ctx, 2)
        to_ctx = ctx if side == 0 else partner
        possible = side == 0 and dx == 0 and dy in (0, 1, -1)
        copy = remote(
            rs_send.at[g, side, pl.ds(b * part, part), :],
            rs_recv.at[place, pl.ds(pl.multiple_of(lo * part, part), part), :],
            rs_ssem.at[g, side, b],
            rs_rsem.at[place],
            ctx=to_ctx,
            req=first_req + core,
        )
        return copy, lo, (first_req + core == req) if possible else None

    def send_terms(g, terms):
        ds_copy(g).wait_recv()
        for side in range(2):
            rs_send[g, side] = (terms[side] + ds_recv[g, side].astype(jnp.float32)).astype(jnp.bfloat16)
        for b in range(blocks):
            for side in (1, 0):
                copy, lo, here = rs_copy(g, b, side)
                if here is None:
                    copy.start()
                else:

                    @pl.when(here)
                    def _():
                        rs_recv[place, pl.ds(pl.multiple_of(lo * part, part), part), :] = rs_send[
                            g, side, pl.ds(b * part, part), :
                        ]

                    @pl.when(jnp.logical_not(here))
                    def _():
                        copy.start()

    def terms_sent(g):
        for b in range(blocks):
            for side in range(2):
                copy, lo, here = rs_copy(g, b, side)
                if here is None:
                    copy.wait_send()
                else:

                    @pl.when(jnp.logical_not(here))
                    def _():
                        copy.wait_send()

    for sub in range(2):
        for offset, link in ARRIVALS[0]:
            tok_copy(offset, link, sub).start()
    token_step(0, 0)
    token_step(0, 1)
    gate_up(0, *whole)
    token_step(1, 0)
    hidden(0, *whole)
    token_step(1, 1)
    gate_up(1, *whole)
    token_step(2, 0)
    hidden(1, *whole)
    pass_on(0, *whole)
    token_step(2, 1)
    gate_up(2, *whole)
    token_step(3, 0)
    hidden(2, *whole)
    pass_on(1, *whole)
    gate_up(3, halves[0])
    token_step(3, 1)
    gate_up(3, halves[1])
    hidden(3, halves[0])
    hidden(3, halves[1])
    for copy in down_copies:
        copy.wait()
    terms = down(0, whole)
    pass_on(2, *whole)
    send_terms(0, terms)
    pass_on(3, halves[0])
    terms = down(1, whole)
    pass_on(3, halves[1])
    send_terms(1, terms)
    terms = down(2, whole)
    send_terms(2, terms)

    def resid_copy(i):
        lo, slot = (y_lo, 0) if i == 0 else (1 - y_lo, 1 + 2 * y_lo)
        return remote(
            tok.at[1 - core, slot],
            resid_out.at[pl.ds(pl.multiple_of(lo * part, part), part), mine],
            resid_sem.at[0, i],
            resid_sem.at[1, i],
            req=sibling,
        )

    for i in range(2):
        resid_copy(i).start()
        lo, slot = (y_lo, 0) if i == 0 else (1 - y_lo, 1 + 2 * y_lo)
        resid_out[pl.ds(pl.multiple_of(lo * part, part), part), mine] = tok[core, slot]

    terms = down(3, halves)
    send_terms(3, terms)

    for dz in FAR_FIRST:
        party_copy(dz).wait_send()
        projy_copy(dz).wait_send()
    for dz in FAR_FIRST[:-1]:
        partz_copy(dz).wait_send()
        projz_copy(dz).wait_send()
        slab_copy(along_z(dz), core, z, core).wait_send()
        slab_copy(along_z(dz), 1 - core, z, core).wait_send()
    slab_copy(z, 1 - core, z, core).wait_send()
    for step in ARRIVALS:
        for offset, link in step:
            for sub in range(2):
                tok_copy(offset, link, sub).wait_send()
    for g in range(CHUNKS):
        for lanes in whole if g + 1 < CHUNKS else halves:
            sib_copy(g, lanes).wait_send()
            hid_sent(g, lanes)
        ds_copy(g).wait_send()
    for i in range(2):
        resid_copy(i).wait()

    def add_terms(s, total):
        there = lax.rem(place + s, 16)
        remote(
            rs_recv.at[there],
            rs_recv.at[there],
            rs_ssem.at[0, 0, 0],
            rs_rsem.at[there],
            ctx=z * 2 + lax.rem(there, 2),
            req=there // 2 * 2 + core,
        ).wait_recv()
        return total + rs_recv[there].astype(jnp.float32)

    total = lax.fori_loop(1, 16, add_terms, rs_recv[place].astype(jnp.float32))
    out[...] = total.astype(jnp.bfloat16)
    for g in range(CHUNKS):
        terms_sent(g)


def layer(
    hidden_in,
    queries,
    suffix_kv,
    prefix_kv,
    hyp_prefix,
    suffix_len,
    prefix_len,
    w_out,
    gain_attn,
    gain_pre,
    w_gate,
    w_up,
    w_down,
):
    n = 16
    nz = 8
    tokens, width = hidden_in.shape
    half = width // 2
    rows = HEADS // KV_HEADS * tokens
    slab = tokens // n
    positions = prefix_kv.shape[1] * prefix_kv.shape[2]
    units = w_gate.shape[1]
    columns = w_down.shape[1]
    chunk = 16 // CHUNKS * tokens // 2
    vmem = pl.BlockSpec(memory_space=pltpu.VMEM)
    smem = pl.BlockSpec(memory_space=pltpu.SMEM)
    hbm = pl.BlockSpec(memory_space=pl.ANY)
    dma = pltpu.SemaphoreType.DMA
    bf16 = jnp.bfloat16
    resid, out = pl.pallas_call(
        layer_kernel,
        out_shape=(
            jax.ShapeDtypeStruct((tokens, width), bf16),
            jax.ShapeDtypeStruct((tokens, columns), bf16),
        ),
        in_specs=[hbm, hbm, hbm, smem, smem, smem, hbm, hbm, vmem, vmem, hbm, hbm, hbm],
        out_specs=(vmem, vmem),
        scratch_shapes=[
            pltpu.VMEM(queries.shape, bf16),
            pltpu.VMEM(suffix_kv.shape, bf16),
            pltpu.VMEM(prefix_kv.shape, bf16),
            pltpu.VMEM(w_out.shape, bf16),
            pltpu.VMEM(hidden_in.shape, bf16),
            pltpu.VMEM((2, width), jnp.float32),
            pltpu.VMEM((rows, positions), jnp.float32),
            pltpu.VMEM((nz, rows + 16, HEAD), bf16),
            pltpu.VMEM((nz, rows + 16, HEAD), bf16),
            pltpu.VMEM((nz, rows + 8, HEAD), jnp.float32),
            pltpu.VMEM((nz, rows + 16, HEAD), bf16),
            pltpu.VMEM((nz, rows + 16, HEAD), bf16),
            pltpu.VMEM((n, slab, width), bf16),
            pltpu.VMEM((nz, slab, width), bf16),
            pltpu.VMEM((nz, slab, width), bf16),
            pltpu.VMEM((nz, slab, width), bf16),
            pltpu.VMEM((2, slab, half), bf16),
            pltpu.VMEM((columns, n * units), bf16),
            pltpu.VMEM((n * units, columns), bf16),
            pltpu.VMEM((nz * units, columns), bf16),
            pltpu.VMEM((nz * units, columns), bf16),
            pltpu.VMEM((4 * units, half), bf16),
            pltpu.VMEM((2, nz, slab, half), bf16),
            pltpu.VMEM((tokens, half), jnp.float32),
            pltpu.VMEM((2, 16, tokens // 2, half), bf16),
            pltpu.VMEM((CHUNKS, 2 * units + 8, 2 * chunk), jnp.float32),
            pltpu.VMEM((CHUNKS, 2 * units + 8, 2 * chunk), jnp.float32),
            pltpu.VMEM((CHUNKS, nz, 2, units, chunk), bf16),
            pltpu.VMEM((CHUNKS, 2, chunk, columns), bf16),
            pltpu.VMEM((CHUNKS, 2, chunk, columns), bf16),
            pltpu.VMEM((CHUNKS, 2, chunk, columns), bf16),
            pltpu.VMEM((16, tokens, columns), bf16),
            dma((8,)),
            dma((2, nz)),
            dma((2, nz)),
            dma((2, nz)),
            dma((2, nz)),
            dma((2, 2)),
            dma((2, 2 + nz)),
            dma((2, nz)),
            dma((2, nz)),
            dma((2, 2, 16)),
            dma((2, CHUNKS + 1)),
            dma((CHUNKS + 1, nz)),
            dma((CHUNKS + 1, nz)),
            dma((2, CHUNKS)),
            dma((CHUNKS, 2, 4)),
            dma((16,)),
        ],
        compiler_params=pltpu.CompilerParams(
            collective_id=0, has_side_effects=True, vmem_limit_bytes=60 * 2**20
        ),
        cost_estimate=pl.CostEstimate(flops=5 * 10**9, bytes_accessed=10**7, transcendentals=10**6),
        name="layer",
    )(
        queries,
        suffix_kv,
        prefix_kv,
        hyp_prefix,
        suffix_len,
        prefix_len,
        w_out,
        hidden_in,
        gain_attn.reshape(-1, 128),
        gain_pre.reshape(-1, 128),
        w_gate.T,
        w_up.T,
        w_down.T,
    )
    return resid, out


def solution(mesh):
    placed = (
        P("req", None),
        P("req", None),
        P(None, "req", None),
        P(None, "req", "ctx", None),
        P("req"),
        P("req"),
        P("req"),
        P("ctx", None),
        P(),
        P(),
        P(None, ("req", "ctx")),
        P(None, ("req", "ctx")),
        P("req", "ctx"),
    )
    return jax.shard_map(
        layer,
        mesh=mesh,
        in_specs=placed,
        out_specs=(P("req", None), P("req", "ctx")),
        check_vma=False,
    )
```

time: 132 us -> 117 us (0.89)
  Pallas kernels: 128 us -> 113 us
    pallas_call x1, Pallas kernels: 128 us -> 113 us  [layer(): pl.pallas_call(layer_kernel, out_shape=(jax.ShapeDtypeStruct((tokens, wid...]
    reshape x1 -> x0, local copies, waits for them, and re-layouts: 2.01 us -> none  [layer(): return (resid.reshape(tokens, width), out)]
    unnamed x1 -> x2, local copies, waits for them, and re-layouts: 1.42 us -> 3.34 us
where the time goes in v4:
time: 117 us
  Pallas kernels  113 us (97%)
  local copies, waits for them, and re-layouts  3.34 us (3%)
    pallas_call x1, Pallas kernels, layer(): pl.pallas_call(layer_kernel, out_shape=(jax.ShapeDtypeStruct((tokens, wid...  113 us
    unnamed x2, local copies, waits for them, and re-layouts  3.34 us

profile of v4, /device:TPU:1, one launch (start us, length us, event | category | flops | bytes accessed | tf_op | source)
XLA Modules:
  0.0 116.7 jit_solution(12825344757333304327)
XLA Ops:
  0.6 112.7 %layer.1 = (bf16[64,4608]{1,0:T(8,128)(2,1)}, bf16[64,288]{1,0:T(8,128)(2,1)}) custom-call(bf16[64,4096]{1,0:T(8,128)(2,1)} %queries_in.1, bf16[2,64,2048]{2,1,0:T(8,128)(2,1)} %suffix_in.1, bf16[2,2,128,2048]{3,2,1,0:T(8,128)(2,1)} %prefix_in.1, s32[4]{0:T(128)} %hyp_prefix.1, s32[4]{0:T(128)} %suffix_len.1, s32[2]{0:T(128)} %prefix_len.1, ...), custom_call_target="tpu_custom_call" | custom-call | flops 5000000000 | bytes 10000000 | tf_op jit(solution)/shard_map/layer/pallas_call | solution.py:734
  113.3 1.9 %copy.17 = bf16[64,4608]{1,0:T(8,128)(2,1)} copy(bf16[64,4608]{1,0:T(8,128)(2,1)} %get-tuple-element.4) | data formatting | bytes 1179648
  115.3 1.4 %copy.18 = bf16[64,288]{1,0:T(8,128)(2,1)} copy(bf16[64,288]{1,0:T(8,128)(2,1)} %get-tuple-element.5) | data formatting | bytes 73728

commit v5 on v4

--- a/solution.py
+++ b/solution.py
@@ -159,8 +159,8 @@
     def greet(there_ctx, there_req):
         pl.semaphore_signal(barrier, inc=1, device_id={"ctx": there_ctx, "req": there_req}, device_id_type=MESH)
 
-    def greet_ctx(s, _):
-        greet(lax.rem(ctx + s, n), req)
+    def greet_z(s, _):
+        greet(along_z(s) * 2 + y_lo, req)
         return 0
 
     def greet_core(s, _):
@@ -177,7 +177,8 @@
 
         return 0
 
-    lax.fori_loop(1, n, greet_ctx, 0)
+    greet(partner, req)
+    lax.fori_loop(1, nz, greet_z, 0)
     lax.fori_loop(0, nz, greet_core, 0)
     lax.fori_loop(1, 16, greet_plane, 0)
 
@@ -265,7 +266,7 @@
     loads[0].wait()
     loads[1].wait()
     lax.fori_loop(0, nz // at_once, others_heads, 0)
-    pl.semaphore_wait(barrier, (n - 1) + nz + 14)
+    pl.semaphore_wait(barrier, 1 + (nz - 1) + nz + 14)
     for dz in FAR_FIRST:
         party_copy(dz).start()
 
@@ -296,14 +297,6 @@
     weights = jnp.where(usable, weights_of(scores), 0.0)
     suf_sum = jnp.dot(weights.astype(jnp.bfloat16), suffix_kv[1, :, own], preferred_element_type=jnp.float32)
     suf_total = jnp.sum(weights, 1, keepdims=True)
-
-    for dz in FAR_FIRST[:-1]:
-        party_copy(dz).wait_recv()
-        summed, flat = load_partial(party_recv.at[dz])
-        store_partial(
-            partz_send.at[dz], summed + part_own[dz, 0:rows, :], flat + part_own[dz, rows : rows + 1, :]
-        )
-        partz_copy(dz).start()
 
     loads[5].wait()
     tile = 128
@@ -324,12 +317,21 @@
         )
         for s in range(nz)
     ]
-    for copy in down_copies[: nz // 2]:
-        copy.start()
     for s in range(nz):
         down_own[s * units : (s + 1) * units, :] = down_rows[
             pl.ds(pl.multiple_of((2 * s + y_lo) * units, units), units), :
         ]
+
+    for dz in FAR_FIRST[:-1]:
+        party_copy(dz).wait_recv()
+        summed, flat = load_partial(party_recv.at[dz])
+        store_partial(
+            partz_send.at[dz], summed + part_own[dz, 0:rows, :], flat + part_own[dz, rows : rows + 1, :]
+        )
+        partz_copy(dz).start()
+
+    for copy in down_copies[:2]:
+        copy.start()
 
     party_copy(0).wait_recv()
     summed, flat = load_partial(party_recv.at[0])
@@ -385,6 +387,9 @@
         projz_send[dz] = both.astype(jnp.bfloat16)
         projz_copy(dz).start()
 
+    for copy in down_copies[2:]:
+        copy.start()
+
     for copy in w_copies:
         copy.wait()
     loads[6].wait()
@@ -417,18 +422,36 @@
             req=req - core + to_core,
         )
 
-    for dz in FAR_FIRST[:-1]:
-        slab_copy(along_z(dz), core, z, core).start()
-        slab_copy(along_z(dz), 1 - core, z, core).start()
+    def send_slabs():
+        for dz in FAR_FIRST[:-1]:
+            slab_copy(along_z(dz), core, z, core).start()
+            slab_copy(along_z(dz), 1 - core, z, core).start()
+
+    def near_slabs():
+        for dz in (1, -1):
+            slab_copy(along_z(dz), core, along_z(dz), 0).wait_recv()
+
+    slabs[core, z] = slab_own[core]
     slab_copy(z, 1 - core, z, core).start()
-    for copy in down_copies[nz // 2 :]:
-        copy.start()
-    slabs[core, z] = slab_own[core]
-    slab_copy(z, 1 - core, z, 1 - core).wait_recv()
-    for dz in FAR_FIRST[:-1]:
-        slab_copy(along_z(dz), core, along_z(dz), core).wait_recv()
-        slab_copy(along_z(dz), core, along_z(dz), 1 - core).wait_recv()
-    for c in range(2):
+
+    @pl.when(core == 0)
+    def _():
+        send_slabs()
+        near_slabs()
+
+    @pl.when(core == 1)
+    def _():
+        near_slabs()
+        send_slabs()
+
+    def gather_slabs(c):
+        for dz in FAR_FIRST[:-1] if c == 1 else (4, 3, 5, 2, 6):
+            slab_copy(along_z(dz), core, along_z(dz), c).wait_recv()
+
+        @pl.when(core != c)
+        def _():
+            slab_copy(z, core, z, c).wait_recv()
+
         for s in range(nz):
             at = (c * nz + s) * slab
             block[at : at + slab, :] = slabs[c, s].astype(jnp.float32)
@@ -462,86 +485,68 @@
             if source <= 4 * step:
                 copy.start()
 
-    def sib_copy(g, lanes):
-        which = CHUNKS - 1 + lanes.start // chunk if lanes.size == chunk else g
-        return remote(
-            sib_send.at[g, :, lanes],
-            sib_recv.at[g, :, lanes],
-            sib_sem.at[0, which],
-            sib_sem.at[1, which],
-            req=sibling,
-        )
-
-    whole = (pl.ds(0, 2 * chunk),)
-    halves = (pl.ds(0, chunk), pl.ds(chunk, chunk))
+    def sib_copy(i):
+        return remote(sib_send.at[i], sib_recv.at[i], sib_sem.at[0, i], sib_sem.at[1, i], req=sibling)
+
     own_part = {}
     ones = jnp.ones((16, half), jnp.bfloat16)
 
-    def gate_up(g, lanes):
-        if lanes.size == chunk:
-            those = tok[lanes.start // chunk, g * blocks : (g + 1) * blocks].reshape(chunk, half)
-        else:
-            those = tok[:, g * blocks : (g + 1) * blocks].reshape(2 * chunk, half)
+    def gate_up(i):
+        those = tok[i % 2, i // 2 * blocks : (i // 2 + 1) * blocks].reshape(chunk, half)
         squares = lax.dot_general(ones, those * those, NT, preferred_element_type=jnp.float32)[:8]
-        sib_send[g, 2 * units :, lanes] = squares
-        sib_send[g, : 2 * units, lanes] = lax.dot_general(
+        sib_send[i, 2 * units :] = squares
+        sib_send[i, : 2 * units] = lax.dot_general(
             w_own[2 * units :, :], those, NT, preferred_element_type=jnp.float32
         )
-        sib_copy(g, lanes).start()
+        sib_copy(i).start()
         products = lax.dot_general(w_own[: 2 * units, :], those, NT, preferred_element_type=jnp.float32)
-        own_part[g, lanes.start] = products, squares
+        own_part[i] = products, squares
 
     major = 1 - 2 * core
 
-    def hid_copy(g, lanes, origin, by, to):
-        c = slice(None) if lanes.size != chunk else lanes.start // chunk
-        which = CHUNKS - 1 + lanes.start // chunk if lanes.size == chunk else g
+    def hid_copy(i, origin, to):
         source = along_z(origin)
-        ref = hid.at[g, source] if lanes.size != chunk else hid.at[g, source, c]
+        ref = hid.at[i // 2, source, i % 2]
         return remote(
             ref,
             ref,
-            hid_ssem.at[which, lax.rem(to - origin + 2 * nz, nz)],
-            hid_rsem.at[which, source],
+            hid_ssem.at[i, lax.rem(to - origin + 2 * nz, nz)],
+            hid_rsem.at[i, source],
             ctx=along_z(to) * 2 + y_lo,
         )
 
-    def hidden(g, lanes):
-        sib_copy(g, lanes).wait_recv()
-        products, squares = own_part[g, lanes.start]
-        both = products + sib_recv[g, : 2 * units, lanes]
-        scale = lax.rsqrt((squares + sib_recv[g, 2 * units :, lanes])[0:1] * (1.0 / width) + eps)
+    def hidden(i):
+        sib_copy(i).wait_recv()
+        products, squares = own_part[i]
+        both = products + sib_recv[i, : 2 * units]
+        scale = lax.rsqrt((squares + sib_recv[i, 2 * units :])[0:1] * (1.0 / width) + eps)
         act = jax.nn.gelu(both[:units] * scale, approximate=True) * (both[units:] * scale)
-        act = act.astype(jnp.bfloat16)
-        for i in range(lanes.size // chunk):
-            hid[g, z, lanes.start // chunk + i] = act[:, i * chunk : (i + 1) * chunk]
+        hid[i // 2, z, i % 2] = act.astype(jnp.bfloat16)
         for to in (2, -2, 1, -1):
-            hid_copy(g, lanes, 0, 0, to).start()
-
-    def pass_on(g, lanes):
+            hid_copy(i, 0, to).start()
+
+    def pass_on(i):
         for way in (1, -1):
-            hid_copy(g, lanes, -2 * way, 0, 0).wait_recv()
+            hid_copy(i, -2 * way, 0).wait_recv()
 
             @pl.when(major == way)
             def _():
-                hid_copy(g, lanes, -2 * way, 0, 2 * way).start()
-
-            hid_copy(g, lanes, -2 * way, 0, way).start()
-
-    def hid_arrive(g, lanes):
+                hid_copy(i, -2 * way, 2 * way).start()
+
+            hid_copy(i, -2 * way, way).start()
+
+    def hid_arrive(i):
         for origin in (-1, 1, -3, 3, 4):
-            hid_copy(g, lanes, origin, 0, 0).wait_recv()
-
-    def hid_sent(g, lanes):
-        for to in (2, -2, 1, -1):
-            hid_copy(g, lanes, 0, 0, to).wait_send()
+            hid_copy(i, origin, 0).wait_recv()
+
+    def hid_sent(i):
         for way in (1, -1):
+            for away in (1, 2, 3):
+                hid_copy(i, 0, way * away).wait_send()
 
             @pl.when(major == way)
             def _():
-                hid_copy(g, lanes, -2 * way, 0, 2 * way).wait_send()
-
-            hid_copy(g, lanes, -2 * way, 0, way).wait_send()
+                hid_copy(i, 0, way * 4).wait_send()
 
     def ds_copy(g):
         return remote(ds_send.at[g], ds_recv.at[g], ds_sem.at[0, g], ds_sem.at[1, g], req=sibling)
@@ -552,9 +557,9 @@
             jnp.dot(act, matrix[...], preferred_element_type=jnp.float32) for matrix in (down_own, down_other)
         ]
 
-    def down(g, all_lanes):
-        for lanes in all_lanes:
-            hid_arrive(g, lanes)
+    def down(g):
+        for i in (2 * g, 2 * g + 1):
+            hid_arrive(i)
         for side, term in enumerate(down_terms(g, 1 - core)):
             ds_send[g, side] = term.astype(jnp.bfloat16)
         ds_copy(g).start()
@@ -610,38 +615,25 @@
                         copy.wait_send()
 
     for sub in range(2):
+        gather_slabs(sub)
         for offset, link in ARRIVALS[0]:
             tok_copy(offset, link, sub).start()
-    token_step(0, 0)
-    token_step(0, 1)
-    gate_up(0, *whole)
-    token_step(1, 0)
-    hidden(0, *whole)
-    token_step(1, 1)
-    gate_up(1, *whole)
-    token_step(2, 0)
-    hidden(1, *whole)
-    pass_on(0, *whole)
-    token_step(2, 1)
-    gate_up(2, *whole)
-    token_step(3, 0)
-    hidden(2, *whole)
-    pass_on(1, *whole)
-    gate_up(3, halves[0])
-    token_step(3, 1)
-    gate_up(3, halves[1])
-    hidden(3, halves[0])
-    hidden(3, halves[1])
-    for copy in down_copies:
-        copy.wait()
-    terms = down(0, whole)
-    pass_on(2, *whole)
-    send_terms(0, terms)
-    pass_on(3, halves[0])
-    terms = down(1, whole)
-    pass_on(3, halves[1])
+    for i in range(2 * CHUNKS):
+        token_step(i // 2, i % 2)
+        gate_up(i)
+        if i >= 2:
+            pass_on(i - 2)
+        hidden(i)
+        if i == 6:
+            for copy in down_copies:
+                copy.wait()
+            first_terms = down(0)
+    send_terms(0, first_terms)
+    terms = down(1)
+    pass_on(6)
     send_terms(1, terms)
-    terms = down(2, whole)
+    terms = down(2)
+    pass_on(7)
     send_terms(2, terms)
 
     def resid_copy(i):
@@ -659,7 +651,7 @@
         lo, slot = (y_lo, 0) if i == 0 else (1 - y_lo, 1 + 2 * y_lo)
         resid_out[pl.ds(pl.multiple_of(lo * part, part), part), mine] = tok[core, slot]
 
-    terms = down(3, halves)
+    terms = down(3)
     send_terms(3, terms)
 
     for dz in FAR_FIRST:
@@ -676,9 +668,9 @@
             for sub in range(2):
                 tok_copy(offset, link, sub).wait_send()
     for g in range(CHUNKS):
-        for lanes in whole if g + 1 < CHUNKS else halves:
-            sib_copy(g, lanes).wait_send()
-            hid_sent(g, lanes)
+        for i in (2 * g, 2 * g + 1):
+            sib_copy(i).wait_send()
+            hid_sent(i)
         ds_copy(g).wait_send()
     for i in range(2):
         resid_copy(i).wait()
@@ -765,8 +757,8 @@
             pltpu.VMEM((2, nz, slab, half), bf16),
             pltpu.VMEM((tokens, half), jnp.float32),
             pltpu.VMEM((2, 16, tokens // 2, half), bf16),
-            pltpu.VMEM((CHUNKS, 2 * units + 8, 2 * chunk), jnp.float32),
-            pltpu.VMEM((CHUNKS, 2 * units + 8, 2 * chunk), jnp.float32),
+            pltpu.VMEM((2 * CHUNKS, 2 * units + 8, chunk), jnp.float32),
+            pltpu.VMEM((2 * CHUNKS, 2 * units + 8, chunk), jnp.float32),
             pltpu.VMEM((CHUNKS, nz, 2, units, chunk), bf16),
             pltpu.VMEM((CHUNKS, 2, chunk, columns), bf16),
             pltpu.VMEM((CHUNKS, 2, chunk, columns), bf16),
@@ -782,9 +774,9 @@
             dma((2, nz)),
             dma((2, nz)),
             dma((2, 2, 16)),
-            dma((2, CHUNKS + 1)),
-            dma((CHUNKS + 1, nz)),
-            dma((CHUNKS + 1, nz)),
+            dma((2, 2 * CHUNKS)),
+            dma((2 * CHUNKS, nz)),
+            dma((2 * CHUNKS, nz)),
             dma((2, CHUNKS)),
             dma((CHUNKS, 2, 4)),
             dma((16,)),

time: 117 us -> 108 us (0.923)
  Pallas kernels: 113 us -> 104 us
    pallas_call x1, Pallas kernels: 113 us -> 104 us  [layer(): pl.pallas_call(layer_kernel, out_shape=(jax.ShapeDtypeStruct((tokens, wid...]
where the time goes in v5:
time: 108 us
  Pallas kernels  104 us (96%)
  local copies, waits for them, and re-layouts  3.34 us (3%)
    pallas_call x1, Pallas kernels, layer(): pl.pallas_call(layer_kernel, out_shape=(jax.ShapeDtypeStruct((tokens, wid...  104 us
    unnamed x2, local copies, waits for them, and re-layouts  3.34 us

profile of v5, /device:TPU:1, one launch (start us, length us, event | category | flops | bytes accessed | tf_op | source)
XLA Modules:
  0.0 107.9 jit_solution(15048779274417192961)
XLA Ops:
  0.6 103.9 %layer.1 = (bf16[64,4608]{1,0:T(8,128)(2,1)}, bf16[64,288]{1,0:T(8,128)(2,1)}) custom-call(bf16[64,4096]{1,0:T(8,128)(2,1)} %queries_in.1, bf16[2,64,2048]{2,1,0:T(8,128)(2,1)} %suffix_in.1, bf16[2,2,128,2048]{3,2,1,0:T(8,128)(2,1)} %prefix_in.1, s32[4]{0:T(128)} %hyp_prefix.1, s32[4]{0:T(128)} %suffix_len.1, s32[2]{0:T(128)} %prefix_len.1, ...), custom_call_target="tpu_custom_call" | custom-call | flops 5000000000 | bytes 10000000 | tf_op jit(solution)/shard_map/layer/pallas_call | solution.py:726
  104.6 1.9 %copy.17 = bf16[64,4608]{1,0:T(8,128)(2,1)} copy(bf16[64,4608]{1,0:T(8,128)(2,1)} %get-tuple-element.4) | data formatting | bytes 1179648
  106.5 1.4 %copy.18 = bf16[64,288]{1,0:T(8,128)(2,1)} copy(bf16[64,288]{1,0:T(8,128)(2,1)} %get-tuple-element.5) | data formatting | bytes 73728

commit v6 on v5

--- a/solution.py
+++ b/solution.py
@@ -618,12 +618,36 @@
         gather_slabs(sub)
         for offset, link in ARRIVALS[0]:
             tok_copy(offset, link, sub).start()
+    for dz in FAR_FIRST:
+        party_copy(dz).wait_send()
+        projy_copy(dz).wait_send()
+    for dz in FAR_FIRST[:-1]:
+        partz_copy(dz).wait_send()
+        projz_copy(dz).wait_send()
+
+    def tok_sent(step, sub):
+        for offset, link in ARRIVALS[step]:
+            tok_copy(offset, link, sub).wait_send()
+
+    def slabs_sent():
+        for dz in FAR_FIRST[:-1]:
+            slab_copy(along_z(dz), core, z, core).wait_send()
+            slab_copy(along_z(dz), 1 - core, z, core).wait_send()
+        slab_copy(z, 1 - core, z, core).wait_send()
+
     for i in range(2 * CHUNKS):
         token_step(i // 2, i % 2)
-        gate_up(i)
         if i >= 2:
             pass_on(i - 2)
+        gate_up(i)
         hidden(i)
+        if i == 1:
+            slabs_sent()
+        if i >= 2:
+            tok_sent((i - 2) // 2, i % 2)
+            sib_copy(i - 2).wait_send()
+        if i >= 5:
+            hid_sent(i - 5)
         if i == 6:
             for copy in down_copies:
                 copy.wait()
@@ -635,6 +659,14 @@
     terms = down(2)
     pass_on(7)
     send_terms(2, terms)
+    for sub in range(2):
+        tok_sent(3, sub)
+    for i in (6, 7):
+        sib_copy(i).wait_send()
+    for i in (3, 4, 5):
+        hid_sent(i)
+    for g in range(3):
+        ds_copy(g).wait_send()
 
     def resid_copy(i):
         lo, slot = (y_lo, 0) if i == 0 else (1 - y_lo, 1 + 2 * y_lo)
@@ -651,29 +683,27 @@
         lo, slot = (y_lo, 0) if i == 0 else (1 - y_lo, 1 + 2 * y_lo)
         resid_out[pl.ds(pl.multiple_of(lo * part, part), part), mine] = tok[core, slot]
 
-    terms = down(3)
-    send_terms(3, terms)
-
-    for dz in FAR_FIRST:
-        party_copy(dz).wait_send()
-        projy_copy(dz).wait_send()
-    for dz in FAR_FIRST[:-1]:
-        partz_copy(dz).wait_send()
-        projz_copy(dz).wait_send()
-        slab_copy(along_z(dz), core, z, core).wait_send()
-        slab_copy(along_z(dz), 1 - core, z, core).wait_send()
-    slab_copy(z, 1 - core, z, core).wait_send()
-    for step in ARRIVALS:
-        for offset, link in step:
-            for sub in range(2):
-                tok_copy(offset, link, sub).wait_send()
-    for g in range(CHUNKS):
-        for i in (2 * g, 2 * g + 1):
-            sib_copy(i).wait_send()
-            hid_sent(i)
-        ds_copy(g).wait_send()
+    for i in (6, 7):
+        hid_arrive(i)
+        terms = down_terms(3, i % 2)
+
+        @pl.when(core != i % 2)
+        def _():
+            for side in range(2):
+                ds_send[3, side] = terms[side].astype(jnp.bfloat16)
+            ds_copy(3).start()
+
+        @pl.when(core == i % 2)
+        def _():
+            send_terms(3, terms)
+
+    for i in (6, 7):
+        hid_sent(i)
+    ds_copy(3).wait_send()
     for i in range(2):
         resid_copy(i).wait()
+    for g in range(CHUNKS):
+        terms_sent(g)
 
     def add_terms(s, total):
         there = lax.rem(place + s, 16)
@@ -689,8 +719,24 @@
 
     total = lax.fori_loop(1, 16, add_terms, rs_recv[place].astype(jnp.float32))
     out[...] = total.astype(jnp.bfloat16)
-    for g in range(CHUNKS):
-        terms_sent(g)
+
+
+def place_kernel(resid, out, resid_out, out_out, held, small, sem):
+    rows = resid.shape[0] // 4
+    loads, stores = [], []
+    for i in range(4):
+        at = pl.ds(i * rows, rows)
+        loads.append(pltpu.make_async_copy(resid.at[at, :], held.at[at, :], sem.at[0, i]))
+        stores.append(pltpu.make_async_copy(held.at[at, :], resid_out.at[at, :], sem.at[1, i]))
+    loads.append(pltpu.make_async_copy(out, small, sem.at[0, 4]))
+    stores.append(pltpu.make_async_copy(small, out_out, sem.at[1, 4]))
+    for load in loads:
+        load.start()
+    for load, store in zip(loads, stores):
+        load.wait()
+        store.start()
+    for store in stores:
+        store.wait()
 
 
 def layer(
@@ -801,7 +847,14 @@
         w_up.T,
         w_down.T,
     )
-    return resid, out
+    return pl.pallas_call(
+        place_kernel,
+        out_shape=(jax.ShapeDtypeStruct(resid.shape, bf16), jax.ShapeDtypeStruct(out.shape, bf16)),
+        in_specs=[hbm, hbm],
+        out_specs=(hbm, hbm),
+        scratch_shapes=[pltpu.VMEM(resid.shape, bf16), pltpu.VMEM(out.shape, bf16), dma((2, 5))],
+        name="place",
+    )(resid, out)
 
 
 def solution(mesh):

time: 108 us -> 106 us (0.981)
  local copies, waits for them, and re-layouts: 3.34 us -> 0 us
    unnamed x2 -> x0, local copies, waits for them, and re-layouts: 3.34 us -> none
    pallas_call x0 -> x1, Pallas kernels: none -> 1.88 us  [layer(): pl.pallas_call(place_kernel, out_shape=(jax.ShapeDtypeStruct(resid.shape,...]
    pallas_call x1, Pallas kernels: 104 us -> 103 us  [layer(): pl.pallas_call(layer_kernel, out_shape=(jax.ShapeDtypeStruct((tokens, wid...]
where the time goes in v6:
time: 106 us; the launch traced here: 105 us
  Pallas kernels  105 us (99%)
    pallas_call x1, Pallas kernels, layer(): pl.pallas_call(layer_kernel, out_shape=(jax.ShapeDtypeStruct((tokens, wid...  103 us

profile of v6, /device:TPU:1, one launch (start us, length us, event | category | flops | bytes accessed | tf_op | source)
XLA Modules:
  0.0 105.4 jit_solution(6785423397225124814)
XLA Ops:
  0.6 102.7 %layer.1 = (bf16[64,4608]{1,0:T(8,128)(2,1)}, bf16[64,288]{1,0:T(8,128)(2,1)}) custom-call(bf16[64,4096]{1,0:T(8,128)(2,1)} %queries_in.1, bf16[2,64,2048]{2,1,0:T(8,128)(2,1)} %suffix_in.1, bf16[2,2,128,2048]{3,2,1,0:T(8,128)(2,1)} %prefix_in.1, s32[4]{0:T(128)} %hyp_prefix.1, s32[4]{0:T(128)} %suffix_len.1, s32[2]{0:T(128)} %prefix_len.1, ...), custom_call_target="tpu_custom_call" | custom-call | flops 5000000000 | bytes 10000000 | tf_op jit(solution)/shard_map/layer/pallas_call | solution.py:772
  103.4 1.9 %place.1 = (bf16[64,4608]{1,0:T(8,128)(2,1)}, bf16[64,288]{1,0:T(8,128)(2,1)}) custom-call(bf16[64,4608]{1,0:T(8,128)(2,1)} %get-tuple-element.4.resid, bf16[64,288]{1,0:T(8,128)(2,1)} %get-tuple-element.5.out), custom_call_target="tpu_custom_call" | custom-call | tf_op jit(solution)/shard_map/place/pallas_call | solution.py:850

commit v7 on v6

--- a/solution.py
+++ b/solution.py
@@ -648,14 +648,15 @@
             sib_copy(i - 2).wait_send()
         if i >= 5:
             hid_sent(i - 5)
-        if i == 6:
+        if i == 5:
             for copy in down_copies:
                 copy.wait()
             first_terms = down(0)
-    send_terms(0, first_terms)
-    terms = down(1)
+        if i == 6:
+            send_terms(0, first_terms)
+            second_terms = down(1)
     pass_on(6)
-    send_terms(1, terms)
+    send_terms(1, second_terms)
     terms = down(2)
     pass_on(7)
     send_terms(2, terms)

time: 106 us -> 105 us (level)
  no operation moved by 1% of the time
where the time goes in v7:
time: 105 us
  Pallas kernels  104 us (99%)
    pallas_call x1, Pallas kernels, layer(): pl.pallas_call(layer_kernel, out_shape=(jax.ShapeDtypeStruct((tokens, wid...  102 us

profile of v7, /device:TPU:1, one launch (start us, length us, event | category | flops | bytes accessed | tf_op | source)
XLA Modules:
  0.0 105.0 jit_solution(18404573780590389182)
XLA Ops:
  0.6 102.3 %layer.1 = (bf16[64,4608]{1,0:T(8,128)(2,1)}, bf16[64,288]{1,0:T(8,128)(2,1)}) custom-call(bf16[64,4096]{1,0:T(8,128)(2,1)} %queries_in.1, bf16[2,64,2048]{2,1,0:T(8,128)(2,1)} %suffix_in.1, bf16[2,2,128,2048]{3,2,1,0:T(8,128)(2,1)} %prefix_in.1, s32[4]{0:T(128)} %hyp_prefix.1, s32[4]{0:T(128)} %suffix_len.1, s32[2]{0:T(128)} %prefix_len.1, ...), custom_call_target="tpu_custom_call" | custom-call | flops 5000000000 | bytes 10000000 | tf_op jit(solution)/shard_map/layer/pallas_call | solution.py:773
  103.0 1.9 %place.1 = (bf16[64,4608]{1,0:T(8,128)(2,1)}, bf16[64,288]{1,0:T(8,128)(2,1)}) custom-call(bf16[64,4608]{1,0:T(8,128)(2,1)} %get-tuple-element.4.resid, bf16[64,288]{1,0:T(8,128)(2,1)} %get-tuple-element.5.out), custom_call_target="tpu_custom_call" | custom-call | tf_op jit(solution)/shard_map/place/pallas_call | solution.py:851
